TPU v7x, 1024 devices: a whole 4x4x32 slice. The times are simulated.
1024 devices in a mesh: row: 32 (over z), col: 32 (over y, x, core).
Axes of the slice: x: 4, y: 4, z: 32, core: 2. Of those that a mesh axis runs over, the one named last changes fastest.
Arguments:
- features: bfloat16 [65536, 256], P(('col', 'row')), may hold values from -6 to 6
- block_rows: int32 [32, 32, 24], P('row', 'col'), may hold values from 0 to 15, as said below
- block_cols: int32 [32, 32, 24], P('row', 'col'), may hold values from 0 to 15
- block_values: bfloat16 [32, 32, 24, 128, 128], P('row', 'col'), may hold values from -0.078125 to 0.078125
- block_count: int32 [32, 32], P('row', 'col'), may hold values from 1 to 24, as said below
- w_first: bfloat16 [256, 256], replicated, may hold values from -0.375 to 0.375
- b_first: float32 [256], replicated, may hold values from -3 to 3
- w_second: bfloat16 [256, 256], replicated, may hold values from -0.375 to 0.375
- b_second: float32 [256], replicated, may hold values from -3 to 3
Outputs:
- embedded: bfloat16 [65536, 256], P(('col', 'row'))
Inputs may be any that keep to these rules, and one draw needn't show every extreme that they name: Within each tile the slots hold distinct (block_rows, block_cols) pairs. Slots at or past block_count hold no part of A. Some tile in every draw has all 24 slots live.
All inputs are finite; a program needn't handle non-finite values.
Results may differ from a plain program's by a relative error of at most 0.0054.
Values may be sent and summed in bfloat16 or wider, within the bound.
No kernel may reach another device: no remote copies, remote signals or barrier semaphores. Data moves between devices by JAX's collectives and lax.ppermute only.
A program may use at most 32 MiB of HBM per device.

v0:
```python
import jax
import jax.numpy as jnp
from jax import lax
from jax.sharding import PartitionSpec as P


def block_sum(values, sel_idx, out_idx, out_blocks, count, panel, transpose):
    block_size = values.shape[-1]
    width = panel.shape[1]
    slots = values.shape[0]
    panel_tiles = panel.reshape(-1, block_size, width)
    picked = panel_tiles[sel_idx]
    pattern = "nji,njd->nid" if transpose else "nij,njd->nid"
    products = jnp.einsum(pattern, values, picked, preferred_element_type=jnp.float32)
    live_slots = jnp.arange(slots, dtype=jnp.int32) < count
    onehot = (
        (out_idx[None, :] == jnp.arange(out_blocks, dtype=jnp.int32)[:, None]) & live_slots[None, :]
    ).astype(jnp.float32)
    summed = jnp.dot(
        onehot,
        products.reshape(slots, block_size * width),
        precision=lax.Precision.HIGHEST,
        preferred_element_type=jnp.float32,
    )
    return summed.reshape(out_blocks * block_size, width)


def per_device(
    features,
    block_rows,
    block_cols,
    block_values,
    block_count,
    w_first,
    b_first,
    w_second,
    b_second,
):
    own_rows = features.shape[0]
    block_size = block_values.shape[-1]
    row_blocks = own_rows * lax.axis_size("col") // block_size
    col_blocks = own_rows * lax.axis_size("row") // block_size
    values = block_values[0, 0]
    rows_here = block_rows[0, 0]
    cols_here = block_cols[0, 0]
    count = block_count[0, 0]
    panel = lax.all_gather(features, "row", axis=0, tiled=True)
    partial_value = block_sum(values, cols_here, rows_here, row_blocks, count, panel, False)
    agg_first = lax.psum_scatter(partial_value, "col", scatter_dimension=0, tiled=True).astype(
        jnp.bfloat16
    )
    hidden_own = jax.nn.relu(
        jnp.dot(agg_first, w_first, preferred_element_type=jnp.float32) + b_first
    ).astype(jnp.bfloat16)
    hidden_rows = lax.all_gather(hidden_own, "col", axis=0, tiled=True)
    second_partial = block_sum(values, rows_here, cols_here, col_blocks, count, hidden_rows, True)
    agg_second = lax.psum_scatter(second_partial, "row", scatter_dimension=0, tiled=True).astype(
        jnp.bfloat16
    )
    return (jnp.dot(agg_second, w_second, preferred_element_type=jnp.float32) + b_second).astype(
        jnp.bfloat16
    )


def solution(mesh):
    placed = (
        P(("col", "row"), None),
        P("row", "col", None),
        P("row", "col", None),
        P("row", "col", None, None, None),
        P("row", "col"),
        P(),
        P(),
        P(),
        P(),
    )
    return jax.shard_map(
        per_device, mesh=mesh, in_specs=placed, out_specs=P(("col", "row"), None), check_vma=False
    )
```

profile of v0, /device:TPU:6, one launch (start us, length us, event | category | flops | bytes accessed | tf_op | source)
XLA Modules:
  0.0 530.3 jit_solution(6746143462537069233)
XLA Ops:
  6.5 0.0 copy-start
  6.5 0.0 all-gather.3.cloned.1.call-start
  6.5 0.7 all-gather.3.cloned.1.call-update
  7.3 0.0 reduce-scatter.3.cloned.1.call-start
  8.0 0.7 fusion.17
  8.6 145.5 %all-gather.3.cloned.1.call-done = bf16[2048,256]{1,0:T(8,128)(2,1)} async-done(((bf16[64,256]{1,0:T(8,128)(2,1)}), bf16[2048,256]{1,0:T(8,128)(2,1)}) %all-gather.3.cloned.1.call-update) | async-done | bytes 1048592 | tf_op jit(solution)/shard_map/all_gather | solution.py:47
  154.2 1.9 gather_fusion
  156.0 0.0 copy-done
  156.0 2.3 convolution_bitcast_fusion.1
  158.3 0.0 copy-start.5
  158.3 3.6 copy.16
  161.9 0.0 copy-done.5
  161.9 3.2 fusion.11
  165.1 1.5 reshape.84
  166.6 0.0 copy-start.1
  166.6 0.0 copy-start.3
  166.6 0.0 reduce-scatter.3.cloned.1.call-update
  166.6 0.0 all-gather.5.cloned.1.call-start
  166.6 123.9 %reduce-scatter.3.cloned.1.call-done = f32[64,256]{1,0:T(8,128)} async-done(((f32[2048,256]{1,0:T(8,128)}), f32[64,256]{1,0:T(8,128)}) %reduce-scatter.3.cloned.1.call-update) | async-done | bytes 65552 | tf_op jit(solution)/shard_map/reduce_scatter | solution.py:49
  290.6 0.0 copy-done.1
  290.6 0.0 copy-done.3
  290.6 1.6 fusion.1
  292.2 0.0 all-gather.5.cloned.1.call-update
  292.2 0.0 reduce-scatter.5.cloned.1.call-start
  292.3 80.9 %all-gather.5.cloned.1.call-done = bf16[2048,256]{1,0:T(8,128)(2,1)} async-done(((bf16[64,256]{1,0:T(8,128)(2,1)}), bf16[2048,256]{1,0:T(8,128)(2,1)}) %all-gather.5.cloned.1.call-update) | async-done | bytes 1048592 | tf_op jit(solution)/shard_map/all_gather | solution.py:55
  373.2 1.9 gather_fusion.1
  375.0 2.3 convolution_bitcast_fusion
  377.3 0.0 copy-start.6
  377.3 3.6 copy.17
  380.9 0.0 copy-done.6
  380.9 3.2 fusion.8
  384.0 1.5 reshape.87
  385.5 0.0 copy-start.2
  385.5 0.0 copy-start.4
  385.5 0.0 reduce-scatter.5.cloned.1.call-update
  385.6 136.6 %reduce-scatter.5.cloned.1.call-done = f32[64,256]{1,0:T(8,128)} async-done(((f32[2048,256]{1,0:T(8,128)}), f32[64,256]{1,0:T(8,128)}) %reduce-scatter.5.cloned.1.call-update) | async-done | bytes 65552 | tf_op jit(solution)/shard_map/reduce_scatter | solution.py:57
  522.1 0.0 copy-done.2
  522.1 0.0 copy-done.4
  522.1 1.6 fusion.2
  (4 shorter events, 0.0 us)
Async XLA Ops:
  6.5 149.5 %copy-start = (bf16[1,1,24,128,128]{4,3,2,1,0:T(8,128)(2,1)S(1)}, bf16[1,1,24,128,128]{4,3,2,1,0:T(8,128)(2,1)}, u32[]{:S(2)}) copy-start(bf16[1,1,24,128,128]{4,3,2,1,0:T(8,128)(2,1)} %param.12) | copy-start | bytes 2359300
  6.5 147.6 %all-gather.3.cloned.1.call-start = ((), (), s32[]{:S(2)}) async-start(), calls=%async_computation.2 | async-start | bytes 1081344 | tf_op jit(solution)/shard_map/all_gather | solution.py:47
  7.3 283.3 %reduce-scatter.3.cloned.1.call-start = ((), (), s32[]{:S(2)}) async-start(), calls=%async_computation.3 | async-start | bytes 2162688 | tf_op jit(solution)/shard_map/reduce_scatter | solution.py:49
  158.3 3.6 copy-start.5
  166.6 124.0 %copy-start.1 = (bf16[256,256]{1,0:T(8,128)(2,1)S(1)}, bf16[256,256]{1,0:T(8,128)(2,1)}, u32[]{:S(2)}) copy-start(bf16[256,256]{1,0:T(8,128)(2,1)} %param.14) | copy-start | bytes 393220
  166.6 124.0 %copy-start.3 = (f32[256]{0:T(256)S(1)}, f32[256]{0:T(256)}, u32[]{:S(2)}) copy-start(f32[256]{0:T(256)} %param.15) | copy-start | bytes 3076
  166.6 206.6 %all-gather.5.cloned.1.call-start = ((), (), s32[]{:S(2)}) async-start(), calls=%async_computation.4 | async-start | bytes 1081344 | tf_op jit(solution)/shard_map/all_gather | solution.py:55
  292.2 229.9 %reduce-scatter.5.cloned.1.call-start = ((), (), s32[]{:S(2)}) async-start(), calls=%async_computation.5 | async-start | bytes 2162688 | tf_op jit(solution)/shard_map/reduce_scatter | solution.py:57
  377.3 3.6 copy-start.6
  385.5 136.6 %copy-start.2 = (bf16[256,256]{1,0:T(8,128)(2,1)S(1)}, bf16[256,256]{1,0:T(8,128)(2,1)}, u32[]{:S(2)}) copy-start(bf16[256,256]{1,0:T(8,128)(2,1)} %param.16) | copy-start | bytes 393220
  385.5 136.6 %copy-start.4 = (f32[256]{0:T(256)S(1)}, f32[256]{0:T(256)}, u32[]{:S(2)}) copy-start(f32[256]{0:T(256)} %param.17) | copy-start | bytes 3076
Sparse Core Ops, SparseCore 0:
  10.0 144.0 all-gather.2
  166.7 123.8 reduce-scatter.2
  294.9 78.2 all-gather.4
  385.7 136.3 reduce-scatter.4
where the time goes:
time: 531 us; the launch traced here: 530 us
  waiting for transfers between devices  488 us (92%)
  matrix products  14.1 us (3%)
  local copies, waits for them, and re-layouts  13.9 us (3%)
  between operations  13.8 us (3%)
    all_gather x1, waiting for transfers between devices, per_device(): panel = lax.all_gather(features, 'row', axis=0, tiled=True)  146 us
    reduce_scatter x1, waiting for transfers between devices, per_device(): lax.psum_scatter(second_partial, 'row', scatter_dimension=0, tiled=True)  137 us
    reduce_scatter x1, waiting for transfers between devices, per_device(): lax.psum_scatter(partial_value, 'col', scatter_dimension=0, tiled=True)  124 us
    all_gather x1, waiting for transfers between devices, per_device(): hidden_rows = lax.all_gather(hidden_own, 'col', axis=0, tiled=True)  80.9 us
  transfers between devices with their start and end apart: 4, of which 4 were waited for; matrix products, arithmetic and copies ran while one was open for 0% of the time, Pallas kernels for 0%

commit v1 on v0

v1 whole, which is shorter than its diff:
```python
import functools

import jax
import jax.numpy as jnp
from jax import lax
from jax.experimental import pallas as pl
from jax.experimental.pallas import tpu as pltpu
from jax.sharding import PartitionSpec as P

ROW, COL = "row", "col"
BF16, F32 = jnp.bfloat16, jnp.float32
VMEM = pl.BlockSpec(memory_space=pltpu.VMEM)
SMEM = pl.BlockSpec(memory_space=pltpu.SMEM)
GROUP = 4
VMEM_LIMIT = 12 * 1024 * 1024
PLACE_ROW, PLACE_COL, COUNT, FIRST = 0, 1, 2, 3


def strided(size, stride):
    return [list(range(first, size, stride)) for first in range(stride)]


def shift(size, by):
    return [(i, (i + by) % size) for i in range(size)]


def hop_two(size):
    return [(i, (i + (2 if i % 2 == 0 else -2)) % size) for i in range(size)]


def swap(size):
    return [(i, i + 1 if i % 2 == 0 else i - 1) for i in range(size)]


def fill_panel(panel, own, other, side):
    half = own.shape[1]
    panel[:, pl.ds(pl.multiple_of(side * half, half), half), :] = own[...]
    panel[:, pl.ds(pl.multiple_of((1 - side) * half, half), half), :] = other[...]


def add_products(panel, acc, facts, from_at, to_at, values, transpose):
    spare = acc.shape[0] - 1
    slots = values.shape[0]
    live = facts[COUNT]
    contract = (((0,), (0,)), ((), ())) if transpose else (((1,), (0,)), ((), ()))

    def step(g, carry):
        base = g * GROUP
        products = [
            lax.dot_general(
                values[base + k], panel[facts[from_at + base + k]], contract, preferred_element_type=F32
            )
            for k in range(GROUP)
        ]
        for k in range(GROUP):
            to = jnp.where(base + k < live, facts[to_at + base + k], spare)
            acc[to] += products[k]
        return carry

    assert slots % GROUP == 0
    lax.fori_loop(0, (live + GROUP - 1) // GROUP, step, 0)


def keep_near_kernel(after, values, bias_0, bias_1, values_out, bias_0_out, bias_1_out):
    del after
    for source, target in ((values, values_out), (bias_0, bias_0_out), (bias_1, bias_1_out)):
        target[...] = source[...]


def first_kernel(facts, values, own, other, keep, send, panel, acc):
    fill_panel(panel, own, other, lax.rem(facts[PLACE_ROW], 2))
    acc[...] = jnp.zeros_like(acc)
    slots = values.shape[0]
    add_products(panel, acc, facts, FIRST + slots, FIRST, values, False)
    chips, half = keep.shape[:2]
    core = lax.rem(facts[PLACE_COL], 2)
    keep[...] = acc[:chips, pl.ds(pl.multiple_of(core * half, half), half), :]
    send[...] = acc[:chips, pl.ds(pl.multiple_of((1 - core) * half, half), half), :]


def second_kernel(facts, values, own, other, keep, up, down, two, panel, acc):
    fill_panel(panel, own, other, lax.rem(facts[PLACE_COL], 2))
    acc[...] = jnp.zeros_like(acc)
    slots = values.shape[0]
    add_products(panel, acc, facts, FIRST, FIRST + slots, values, True)
    quads, half = keep.shape[:2]
    for ref, by in ((keep, 0), (up, 1), (down, 3), (two, 2)):
        r = lax.rem(facts[PLACE_ROW] + by, 4)
        offset = pl.multiple_of(lax.rem(r, 2) * half, half)
        for k in range(quads):
            ref[k] = acc[2 * k + r // 2, pl.ds(offset, half), :].astype(ref.dtype)


def dense_kernel(layer, parts, weight, bias, out):
    total = jnp.sum(parts[...].astype(F32), axis=0).astype(BF16)
    result = jnp.dot(total, weight[...], preferred_element_type=F32) + bias[...]
    if layer == 0:
        result = jnp.maximum(result, 0.0)
    result = result.astype(BF16)
    if len(out.shape) == 3:
        for k in range(out.shape[0]):
            out[k] = result
    else:
        out[...] = result


def call(kernel, out_shape, in_specs, scratch=()):
    return pl.pallas_call(
        kernel,
        out_shape=out_shape,
        in_specs=in_specs,
        out_specs=jax.tree.map(lambda _: VMEM, out_shape),
        scratch_shapes=list(scratch),
        compiler_params=pltpu.CompilerParams(vmem_limit_bytes=VMEM_LIMIT),
    )


def shape(dims, dtype):
    return jax.ShapeDtypeStruct(dims, dtype)


def per_device(
    features,
    block_rows,
    block_cols,
    block_values,
    block_count,
    w_first,
    b_first,
    w_second,
    b_second,
):
    rows, cols = lax.axis_size(ROW), lax.axis_size(COL)
    own_rows, width = features.shape
    block = block_values.shape[-1]
    values = block_values[0, 0]
    row_blocks = own_rows * cols // block
    col_blocks = own_rows * rows // block
    scratch = (
        pltpu.VMEM((col_blocks, block, width), BF16),
        pltpu.VMEM((row_blocks + 1, block, width), F32),
    )
    place = jnp.stack([lax.axis_index(ROW), lax.axis_index(COL)]).astype(jnp.int32)
    facts = jnp.concatenate([place, block_count[0], block_rows[0, 0], block_cols[0, 0]])
    chips, quads = cols // 2, rows // 4

    same = lax.all_gather(features, ROW, axis_index_groups=strided(rows, 2))
    other = lax.ppermute(same, ROW, swap(rows))
    piece = (chips, own_rows, width)
    bias_shape = (1, width)
    near = (shape(values.shape, BF16), shape(bias_shape, F32), shape(bias_shape, F32))
    values, bias_first, bias_second = call(keep_near_kernel, near, [VMEM] * 4)(
        same, values, b_first.reshape(bias_shape), b_second.reshape(bias_shape)
    )
    keep, send = call(
        first_kernel, (shape(piece, F32), shape(piece, F32)), [SMEM] + [VMEM] * 3, scratch
    )(facts, values, same, other)

    summed = (keep + lax.ppermute(send, COL, swap(cols))).astype(BF16)
    terms = lax.all_to_all(summed, COL, 0, 0, axis_index_groups=strided(cols, 2))
    copies = call(functools.partial(dense_kernel, 0), shape(piece, BF16), [VMEM] * 3)(
        terms, w_first, bias_first
    )

    mine = lax.all_to_all(copies, COL, 0, 0, axis_index_groups=strided(cols, 2))
    other = lax.ppermute(mine, COL, swap(cols))
    piece = (quads, own_rows, width)
    keep, up, down, two = call(
        second_kernel,
        (shape(piece, F32), shape(piece, BF16), shape(piece, BF16), shape(piece, BF16)),
        [SMEM] + [VMEM] * 3,
        scratch,
    )(facts, values, mine, other)

    two = lax.ppermute(two, ROW, hop_two(rows))
    up = lax.ppermute(up, ROW, shift(rows, 1))
    down = lax.ppermute(down, ROW, shift(rows, -1))
    summed = (keep + up.astype(F32) + down.astype(F32) + two.astype(F32)).astype(BF16)
    terms = lax.all_to_all(summed, ROW, 0, 0, axis_index_groups=strided(rows, 4))
    return call(functools.partial(dense_kernel, 1), shape((own_rows, width), BF16), [VMEM] * 3)(
        terms, w_second, bias_second
    )


def solution(mesh):
    placed = (
        P((COL, ROW), None),
        P(ROW, COL, None),
        P(ROW, COL, None),
        P(ROW, COL, None, None, None),
        P(ROW, COL),
        P(),
        P(),
        P(),
        P(),
    )
    return jax.shard_map(
        per_device, mesh=mesh, in_specs=placed, out_specs=P((COL, ROW), None), check_vma=False
    )
```

time: 531 us -> 178 us (0.34)
  the two profiles are of different devices: /device:TPU:6 before, /device:TPU:22 now
where the time goes in v1:
time: 178 us; the launch traced here: 177 us
  blocking collectives  134 us (75%)
  waiting for transfers between devices  19.5 us (11%)
  starting transfers between devices  15.4 us (9%)
  Pallas kernels  4.31 us (2%)
  local copies, waits for them, and re-layouts  2.55 us (1%)
    all_to_all x1, blocking collectives, per_device(): lax.all_to_all(summed, ROW, 0, 0, axis_index_groups=strided(rows, 4))  54.6 us
    all_gather x1, blocking collectives, per_device(): same = lax.all_gather(features, ROW, axis_index_groups=strided(rows, 2))  51.2 us
    all_to_all x1, blocking collectives, per_device(): lax.all_to_all(summed, COL, 0, 0, axis_index_groups=strided(cols, 2))  14.6 us
    all_to_all x1, blocking collectives, per_device(): mine = lax.all_to_all(copies, COL, 0, 0, axis_index_groups=strided(cols, 2))  14 us
    ppermute x1, waiting for transfers between devices, per_device(): down = lax.ppermute(down, ROW, shift(rows, -1))  6.83 us
    ppermute x1, waiting for transfers between devices, per_device(): other = lax.ppermute(same, ROW, swap(rows))  5.16 us
    ppermute x1, starting transfers between devices, per_device(): down = lax.ppermute(down, ROW, shift(rows, -1))  4.2 us
  transfers between devices with their start and end apart: 6, of which 6 were waited for; matrix products, arithmetic and copies ran while one was open for 0% of the time, Pallas kernels for 0%

profile of v1, /device:TPU:22, one launch (start us, length us, event | category | flops | bytes accessed | tf_op | source)
XLA Modules:
  0.0 177.4 jit_solution(7971825596679551075)
XLA Ops:
  0.0 51.2 %all-gather = bf16[1024,256]{1,0:T(8,128)(2,1)S(1)} all-gather(bf16[64,256]{1,0:T(8,128)(2,1)} %param.9), channel_id=2, replica_groups={{0,64,128,192,256,320,384,448,512,576,640,704,768,832,896,960},{32,96,1..., dimensions={0}, use_global_device_ids=true | all-gather | bytes 557056 | tf_op jit(solution)/shard_map/all_gather | solution.py:147
  51.2 2.6 %collective-permute-start = (bf16[16,64,256]{2,1,0:T(8,128)(2,1)S(1)}, bf16[16,64,256]{2,1,0:T(8,128)(2,1)S(1)}, u32[]{:S(2)}, u32[]{:S(2)}) collective-permute-start(bf16[16,64,256]{2,1,0:T(8,128)(2,1)S(1)} %bitcast.10), channel_id=1, source_target_pairs={{0,32},{32,0},{64,96},{96,64},{128,160},{160,128},{192,224},{224,1... | collective-permute-start | bytes 1572872 | tf_op jit(solution)/shard_map/ppermute | solution.py:148
  53.8 0.0 copy-start.4
  54.5 0.0 copy-start.3
  54.5 0.0 copy-done.4
  54.5 0.7 copy-done.3
  55.1 0.0 copy-start
  55.1 1.1 copy-done
  56.3 0.1 shard_map.91
  56.3 0.0 copy-start.5
  56.3 0.0 copy-start.6
  56.4 0.6 copy-done.5
  57.0 0.0 copy-done.6
  57.0 0.1 concatenate.3.facts
  57.1 5.2 %collective-permute-done.other = bf16[16,64,256]{2,1,0:T(8,128)(2,1)S(1)} collective-permute-done((bf16[16,64,256]{2,1,0:T(8,128)(2,1)S(1)}, bf16[16,64,256]{2,1,0:T(8,128)(2,1)S(1)}, u32[]{:S(2)}, u32[]{:S(2)}) %collective-permute-start) | collective-permute-done | bytes 524320 | tf_op jit(solution)/shard_map/ppermute | solution.py:148
  62.2 1.6 shard_map.92
  63.8 1.9 %collective-permute-start.1 = (f32[16,64,256]{2,1,0:T(8,128)S(1)}, f32[16,64,256]{2,1,0:T(8,128)S(1)}, u32[]{:S(2)}, u32[]{:S(2)}) collective-permute-start(f32[16,64,256]{2,1,0:T(8,128)S(1)} %get-tuple-element.16), channel_id=1, source_target_pairs={{0,1},{1,0},{2,3},{3,2},{4,5},{5,4},{6,7},{7,6},{8,9},{9,8},{10,11... | collective-permute-start | bytes 3145736 | tf_op jit(solution)/shard_map/ppermute | solution.py:159
  65.8 2.6 %collective-permute-done.1 = f32[16,64,256]{2,1,0:T(8,128)S(1)} collective-permute-done((f32[16,64,256]{2,1,0:T(8,128)S(1)}, f32[16,64,256]{2,1,0:T(8,128)S(1)}, u32[]{:S(2)}, u32[]{:S(2)}) %collective-permute-start.1) | collective-permute-done | bytes 1048608 | tf_op jit(solution)/shard_map/ppermute | solution.py:159
  68.4 0.2 add_convert_fusion
  68.6 0.0 copy-start.2
  68.6 14.6 %all_to_all.15.parts = bf16[16,64,256]{2,1,0:T(8,128)(2,1)S(1)} all-to-all(bf16[16,64,256]{2,1,0:T(8,128)(2,1)S(1)} %add_convert_fusion), channel_id=1, replica_groups={{0,2,4,6,8,10,12,14,16,18,20,22,24,26,28,30},{1,3,5,7,9,11,13,15,17,19,..., dimensions={0} | all-to-all | bytes 1048576 | tf_op jit(solution)/shard_map/all_to_all | solution.py:160
  83.2 0.0 copy-done.2
  83.2 0.2 shard_map.93
  83.5 14.0 %all_to_all.16.own = bf16[16,64,256]{2,1,0:T(8,128)(2,1)S(1)} all-to-all(bf16[16,64,256]{2,1,0:T(8,128)(2,1)S(1)} %shard_map.93), channel_id=1, replica_groups={{0,2,4,6,8,10,12,14,16,18,20,22,24,26,28,30},{1,3,5,7,9,11,13,15,17,19,..., dimensions={0} | all-to-all | bytes 1048576 | tf_op jit(solution)/shard_map/all_to_all | solution.py:165
  97.5 1.9 %collective-permute-start.2 = (bf16[16,64,256]{2,1,0:T(8,128)(2,1)S(1)}, bf16[16,64,256]{2,1,0:T(8,128)(2,1)S(1)}, u32[]{:S(2)}, u32[]{:S(2)}) collective-permute-start(bf16[16,64,256]{2,1,0:T(8,128)(2,1)S(1)} %all_to_all.16.own), channel_id=1, source_target_pairs={{0,1},{1,0},{2,3},{3,2},{4,5},{5,4},{6,7},{7,6},{8,9},{9,8},{10,11... | collective-permute-start | bytes 1572872 | tf_op jit(solution)/shard_map/ppermute | solution.py:166
  99.4 1.9 %collective-permute-done.2.other = bf16[16,64,256]{2,1,0:T(8,128)(2,1)S(1)} collective-permute-done((bf16[16,64,256]{2,1,0:T(8,128)(2,1)S(1)}, bf16[16,64,256]{2,1,0:T(8,128)(2,1)S(1)}, u32[]{:S(2)}, u32[]{:S(2)}) %collective-permute-start.2) | collective-permute-done | bytes 524320 | tf_op jit(solution)/shard_map/ppermute | solution.py:166
  101.3 1.7 shard_map.94
  102.9 2.9 %collective-permute-start.3 = (bf16[8,64,256]{2,1,0:T(8,128)(2,1)S(1)}, bf16[8,64,256]{2,1,0:T(8,128)(2,1)S(1)}, u32[]{:S(2)}, u32[]{:S(2)}) collective-permute-start(bf16[8,64,256]{2,1,0:T(8,128)(2,1)S(1)} %get-tuple-element.19), channel_id=1, source_target_pairs={{0,32},{32,64},{64,96},{96,128},{128,160},{160,192},{192,224},{224... | collective-permute-start | bytes 786440 | tf_op jit(solution)/shard_map/ppermute | solution.py:176
  105.8 4.2 %collective-permute-start.4 = (bf16[8,64,256]{2,1,0:T(8,128)(2,1)S(1)}, bf16[8,64,256]{2,1,0:T(8,128)(2,1)S(1)}, u32[]{:S(2)}, u32[]{:S(2)}) collective-permute-start(bf16[8,64,256]{2,1,0:T(8,128)(2,1)S(1)} %get-tuple-element.20), channel_id=1, source_target_pairs={{0,992},{32,0},{64,32},{96,64},{128,96},{160,128},{192,160},{224,1... | collective-permute-start | bytes 786440 | tf_op jit(solution)/shard_map/ppermute | solution.py:177
  110.0 1.9 %collective-permute-start.5 = (bf16[8,64,256]{2,1,0:T(8,128)(2,1)S(1)}, bf16[8,64,256]{2,1,0:T(8,128)(2,1)S(1)}, u32[]{:S(2)}, u32[]{:S(2)}) collective-permute-start(bf16[8,64,256]{2,1,0:T(8,128)(2,1)S(1)} %get-tuple-element.21), channel_id=1, source_target_pairs={{0,64},{32,992},{64,128},{96,32},{128,192},{160,96},{192,256},{224... | collective-permute-start | bytes 786440 | tf_op jit(solution)/shard_map/ppermute | solution.py:175
  111.9 2.5 %collective-permute-done.3 = bf16[8,64,256]{2,1,0:T(8,128)(2,1)S(1)} collective-permute-done((bf16[8,64,256]{2,1,0:T(8,128)(2,1)S(1)}, bf16[8,64,256]{2,1,0:T(8,128)(2,1)S(1)}, u32[]{:S(2)}, u32[]{:S(2)}) %collective-permute-start.3) | collective-permute-done | bytes 262176 | tf_op jit(solution)/shard_map/ppermute | solution.py:176
  114.4 6.8 %collective-permute-done.4 = bf16[8,64,256]{2,1,0:T(8,128)(2,1)S(1)} collective-permute-done((bf16[8,64,256]{2,1,0:T(8,128)(2,1)S(1)}, bf16[8,64,256]{2,1,0:T(8,128)(2,1)S(1)}, u32[]{:S(2)}, u32[]{:S(2)}) %collective-permute-start.4) | collective-permute-done | bytes 262176 | tf_op jit(solution)/shard_map/ppermute | solution.py:177
  121.2 0.6 collective-permute-done.5
  121.8 0.1 add_convert_fusion.1
  121.9 0.0 copy-start.1
  121.9 54.6 %all_to_all.17.parts = bf16[8,64,256]{2,1,0:T(8,128)(2,1)S(1)} all-to-all(bf16[8,64,256]{2,1,0:T(8,128)(2,1)S(1)} %add_convert_fusion.1), channel_id=1, replica_groups={{0,128,256,384,512,640,768,896},{32,160,288,416,544,672,800,928},{64,19..., dimensions={0} | all-to-all | bytes 524288 | tf_op jit(solution)/shard_map/all_to_all | solution.py:179
  176.6 0.0 copy-done.1
  176.6 0.8 shard_map.95
Async XLA Ops:
  51.2 11.1 %collective-permute-start = (bf16[16,64,256]{2,1,0:T(8,128)(2,1)S(1)}, bf16[16,64,256]{2,1,0:T(8,128)(2,1)S(1)}, u32[]{:S(2)}, u32[]{:S(2)}) collective-permute-start(bf16[16,64,256]{2,1,0:T(8,128)(2,1)S(1)} %bitcast.10), channel_id=1, source_target_pairs={{0,32},{32,0},{64,96},{96,64},{128,160},{160,128},{192,224},{224,1... | collective-permute-start | bytes 1572872 | tf_op jit(solution)/shard_map/ppermute | solution.py:148
  53.8 0.7 copy-start.4
  54.5 0.7 copy-start.3
  55.1 1.1 copy-start
  56.3 0.7 copy-start.5
  56.3 0.7 copy-start.6
  63.8 4.6 %collective-permute-start.1 = (f32[16,64,256]{2,1,0:T(8,128)S(1)}, f32[16,64,256]{2,1,0:T(8,128)S(1)}, u32[]{:S(2)}, u32[]{:S(2)}) collective-permute-start(f32[16,64,256]{2,1,0:T(8,128)S(1)} %get-tuple-element.16), channel_id=1, source_target_pairs={{0,1},{1,0},{2,3},{3,2},{4,5},{5,4},{6,7},{7,6},{8,9},{9,8},{10,11... | collective-permute-start | bytes 3145736 | tf_op jit(solution)/shard_map/ppermute | solution.py:159
  68.6 14.6 %copy-start.2 = (bf16[256,256]{1,0:T(8,128)(2,1)S(1)}, bf16[256,256]{1,0:T(8,128)(2,1)}, u32[]{:S(2)}) copy-start(bf16[256,256]{1,0:T(8,128)(2,1)} %weight.2) | copy-start | bytes 393220
  97.5 3.8 %collective-permute-start.2 = (bf16[16,64,256]{2,1,0:T(8,128)(2,1)S(1)}, bf16[16,64,256]{2,1,0:T(8,128)(2,1)S(1)}, u32[]{:S(2)}, u32[]{:S(2)}) collective-permute-start(bf16[16,64,256]{2,1,0:T(8,128)(2,1)S(1)} %all_to_all.16.own), channel_id=1, source_target_pairs={{0,1},{1,0},{2,3},{3,2},{4,5},{5,4},{6,7},{7,6},{8,9},{9,8},{10,11... | collective-permute-start | bytes 1572872 | tf_op jit(solution)/shard_map/ppermute | solution.py:166
  102.9 11.5 %collective-permute-start.3 = (bf16[8,64,256]{2,1,0:T(8,128)(2,1)S(1)}, bf16[8,64,256]{2,1,0:T(8,128)(2,1)S(1)}, u32[]{:S(2)}, u32[]{:S(2)}) collective-permute-start(bf16[8,64,256]{2,1,0:T(8,128)(2,1)S(1)} %get-tuple-element.19), channel_id=1, source_target_pairs={{0,32},{32,64},{64,96},{96,128},{128,160},{160,192},{192,224},{224... | collective-permute-start | bytes 786440 | tf_op jit(solution)/shard_map/ppermute | solution.py:176
  105.8 15.4 %collective-permute-start.4 = (bf16[8,64,256]{2,1,0:T(8,128)(2,1)S(1)}, bf16[8,64,256]{2,1,0:T(8,128)(2,1)S(1)}, u32[]{:S(2)}, u32[]{:S(2)}) collective-permute-start(bf16[8,64,256]{2,1,0:T(8,128)(2,1)S(1)} %get-tuple-element.20), channel_id=1, source_target_pairs={{0,992},{32,0},{64,32},{96,64},{128,96},{160,128},{192,160},{224,1... | collective-permute-start | bytes 786440 | tf_op jit(solution)/shard_map/ppermute | solution.py:177
  110.0 11.8 %collective-permute-start.5 = (bf16[8,64,256]{2,1,0:T(8,128)(2,1)S(1)}, bf16[8,64,256]{2,1,0:T(8,128)(2,1)S(1)}, u32[]{:S(2)}, u32[]{:S(2)}) collective-permute-start(bf16[8,64,256]{2,1,0:T(8,128)(2,1)S(1)} %get-tuple-element.21), channel_id=1, source_target_pairs={{0,64},{32,992},{64,128},{96,32},{128,192},{160,96},{192,256},{224... | collective-permute-start | bytes 786440 | tf_op jit(solution)/shard_map/ppermute | solution.py:175
  121.9 54.7 %copy-start.1 = (bf16[256,256]{1,0:T(8,128)(2,1)S(1)}, bf16[256,256]{1,0:T(8,128)(2,1)}, u32[]{:S(2)}) copy-start(bf16[256,256]{1,0:T(8,128)(2,1)} %weight.3) | copy-start | bytes 393220

commit v2 on v1

--- a/solution.py
+++ b/solution.py
@@ -78,13 +78,13 @@
     send[...] = acc[:chips, pl.ds(pl.multiple_of((1 - core) * half, half), half), :]
 
 
-def second_kernel(facts, values, own, other, keep, up, down, two, panel, acc):
+def second_kernel(facts, values, own, other, keep, two, up, down, panel, acc):
     fill_panel(panel, own, other, lax.rem(facts[PLACE_COL], 2))
     acc[...] = jnp.zeros_like(acc)
     slots = values.shape[0]
     add_products(panel, acc, facts, FIRST, FIRST + slots, values, True)
     quads, half = keep.shape[:2]
-    for ref, by in ((keep, 0), (up, 1), (down, 3), (two, 2)):
+    for ref, by in ((two, 2), (up, 1), (down, 3), (keep, 0)):
         r = lax.rem(facts[PLACE_ROW] + by, 4)
         offset = pl.multiple_of(lax.rem(r, 2) * half, half)
         for k in range(quads):
@@ -165,7 +165,7 @@
     mine = lax.all_to_all(copies, COL, 0, 0, axis_index_groups=strided(cols, 2))
     other = lax.ppermute(mine, COL, swap(cols))
     piece = (quads, own_rows, width)
-    keep, up, down, two = call(
+    keep, two, up, down = call(
         second_kernel,
         (shape(piece, F32), shape(piece, BF16), shape(piece, BF16), shape(piece, BF16)),
         [SMEM] + [VMEM] * 3,
@@ -175,7 +175,7 @@
     two = lax.ppermute(two, ROW, hop_two(rows))
     up = lax.ppermute(up, ROW, shift(rows, 1))
     down = lax.ppermute(down, ROW, shift(rows, -1))
-    summed = (keep + up.astype(F32) + down.astype(F32) + two.astype(F32)).astype(BF16)
+    summed = (keep + two.astype(F32) + up.astype(F32) + down.astype(F32)).astype(BF16)
     terms = lax.all_to_all(summed, ROW, 0, 0, axis_index_groups=strided(rows, 4))
     return call(functools.partial(dense_kernel, 1), shape((own_rows, width), BF16), [VMEM] * 3)(
         terms, w_second, bias_second

time: 178 us -> 177 us (level)
  the two profiles are of different devices: /device:TPU:22 before, /device:TPU:1 now
where the time goes in v2:
time: 177 us
  blocking collectives  125 us (71%)
  starting transfers between devices  25.1 us (14%)
  waiting for transfers between devices  17.2 us (10%)
  Pallas kernels  5.8 us (3%)
  local copies, waits for them, and re-layouts  2.55 us (1%)
    all_to_all x1, blocking collectives, per_device(): lax.all_to_all(summed, ROW, 0, 0, axis_index_groups=strided(rows, 4))  49.1 us
    all_gather x1, blocking collectives, per_device(): same = lax.all_gather(features, ROW, axis_index_groups=strided(rows, 2))  45.2 us
    all_to_all x1, blocking collectives, per_device(): lax.all_to_all(summed, COL, 0, 0, axis_index_groups=strided(cols, 2))  17.5 us
    all_to_all x1, blocking collectives, per_device(): mine = lax.all_to_all(copies, COL, 0, 0, axis_index_groups=strided(cols, 2))  13.4 us
    ppermute x1, starting transfers between devices, per_device(): summed = (keep + lax.ppermute(send, COL, swap(cols))).astype(BF16)  9.85 us
    ppermute x1, waiting for transfers between devices, per_device(): up = lax.ppermute(up, ROW, shift(rows, 1))  5.55 us
    ppermute x1, starting transfers between devices, per_device(): other = lax.ppermute(mine, COL, swap(cols))  4.23 us
    ppermute x1, waiting for transfers between devices, per_device(): other = lax.ppermute(same, ROW, swap(rows))  3.98 us
  transfers between devices with their start and end apart: 6, of which 5 were waited for; matrix products, arithmetic and copies ran while one was open for 0% of the time, Pallas kernels for 0%

profile of v2, /device:TPU:1, one launch (start us, length us, event | category | flops | bytes accessed | tf_op | source)
XLA Modules:
  0.0 177.0 jit_solution(6350120714642446711)
XLA Ops:
  0.0 45.2 %all-gather = bf16[1024,256]{1,0:T(8,128)(2,1)S(1)} all-gather(bf16[64,256]{1,0:T(8,128)(2,1)} %param.9), channel_id=2, replica_groups={{0,64,128,192,256,320,384,448,512,576,640,704,768,832,896,960},{32,96,1..., dimensions={0}, use_global_device_ids=true | all-gather | bytes 557056 | tf_op jit(solution)/shard_map/all_gather | solution.py:147
  45.2 2.6 %collective-permute-start = (bf16[16,64,256]{2,1,0:T(8,128)(2,1)S(1)}, bf16[16,64,256]{2,1,0:T(8,128)(2,1)S(1)}, u32[]{:S(2)}, u32[]{:S(2)}) collective-permute-start(bf16[16,64,256]{2,1,0:T(8,128)(2,1)S(1)} %bitcast.10), channel_id=1, source_target_pairs={{0,32},{32,0},{64,96},{96,64},{128,160},{160,128},{192,224},{224,1... | collective-permute-start | bytes 1572872 | tf_op jit(solution)/shard_map/ppermute | solution.py:148
  47.8 0.0 copy-start.4
  48.5 0.0 copy-start.3
  48.5 0.0 copy-done.4
  48.5 0.7 copy-done.3
  49.2 0.0 copy-start
  49.2 1.1 copy-done
  50.3 0.1 shard_map.91
  50.4 0.0 copy-start.5
  50.4 0.0 copy-start.6
  50.4 0.6 copy-done.5
  51.0 0.0 copy-done.6
  51.1 0.1 concatenate.3.facts
  51.1 4.0 %collective-permute-done.other = bf16[16,64,256]{2,1,0:T(8,128)(2,1)S(1)} collective-permute-done((bf16[16,64,256]{2,1,0:T(8,128)(2,1)S(1)}, bf16[16,64,256]{2,1,0:T(8,128)(2,1)S(1)}, u32[]{:S(2)}, u32[]{:S(2)}) %collective-permute-start) | collective-permute-done | bytes 524320 | tf_op jit(solution)/shard_map/ppermute | solution.py:148
  55.1 2.3 %shard_map.92 = (f32[16,64,256]{2,1,0:T(8,128)S(1)}, f32[16,64,256]{2,1,0:T(8,128)S(1)}) custom-call(s32[51]{0:T(128)S(1)} %concatenate.3.facts, bf16[24,128,128]{2,1,0:T(8,128)(2,1)S(1)} %get-tuple-element.14.values, bf16[16,64,256]{2,1,0:T(8,128)(2,1)S(1)} %bitcast.12, bf16[16,64,256]{2,1,0:T(8,128)(2,1)S(1)} %collective-permute-done.other), custom_call_target="tpu_custom_call" | custom-call | tf_op jit(solution)/shard_map/pallas_call | solution.py:155
  57.4 9.9 %collective-permute-start.1 = (f32[16,64,256]{2,1,0:T(8,128)S(1)}, f32[16,64,256]{2,1,0:T(8,128)S(1)}, u32[]{:S(2)}, u32[]{:S(2)}) collective-permute-start(f32[16,64,256]{2,1,0:T(8,128)S(1)} %get-tuple-element.16), channel_id=1, source_target_pairs={{0,1},{1,0},{2,3},{3,2},{4,5},{5,4},{6,7},{7,6},{8,9},{9,8},{10,11... | collective-permute-start | bytes 3145736 | tf_op jit(solution)/shard_map/ppermute | solution.py:159
  67.2 2.3 %collective-permute-done.1 = f32[16,64,256]{2,1,0:T(8,128)S(1)} collective-permute-done((f32[16,64,256]{2,1,0:T(8,128)S(1)}, f32[16,64,256]{2,1,0:T(8,128)S(1)}, u32[]{:S(2)}, u32[]{:S(2)}) %collective-permute-start.1) | collective-permute-done | bytes 1048608 | tf_op jit(solution)/shard_map/ppermute | solution.py:159
  69.5 0.2 add_convert_fusion
  69.7 0.0 copy-start.2
  69.7 17.5 %all_to_all.15.parts = bf16[16,64,256]{2,1,0:T(8,128)(2,1)S(1)} all-to-all(bf16[16,64,256]{2,1,0:T(8,128)(2,1)S(1)} %add_convert_fusion), channel_id=1, replica_groups={{0,2,4,6,8,10,12,14,16,18,20,22,24,26,28,30},{1,3,5,7,9,11,13,15,17,19,..., dimensions={0} | all-to-all | bytes 1048576 | tf_op jit(solution)/shard_map/all_to_all | solution.py:160
  87.2 0.0 copy-done.2
  87.2 0.2 shard_map.93
  87.4 13.4 %all_to_all.16.own = bf16[16,64,256]{2,1,0:T(8,128)(2,1)S(1)} all-to-all(bf16[16,64,256]{2,1,0:T(8,128)(2,1)S(1)} %shard_map.93), channel_id=1, replica_groups={{0,2,4,6,8,10,12,14,16,18,20,22,24,26,28,30},{1,3,5,7,9,11,13,15,17,19,..., dimensions={0} | all-to-all | bytes 1048576 | tf_op jit(solution)/shard_map/all_to_all | solution.py:165
  100.9 4.2 %collective-permute-start.2 = (bf16[16,64,256]{2,1,0:T(8,128)(2,1)S(1)}, bf16[16,64,256]{2,1,0:T(8,128)(2,1)S(1)}, u32[]{:S(2)}, u32[]{:S(2)}) collective-permute-start(bf16[16,64,256]{2,1,0:T(8,128)(2,1)S(1)} %all_to_all.16.own), channel_id=1, source_target_pairs={{0,1},{1,0},{2,3},{3,2},{4,5},{5,4},{6,7},{7,6},{8,9},{9,8},{10,11... | collective-permute-start | bytes 1572872 | tf_op jit(solution)/shard_map/ppermute | solution.py:166
  105.1 1.5 collective-permute-done.2.other
  106.6 2.5 %shard_map.94 = (f32[8,64,256]{2,1,0:T(8,128)S(1)}, bf16[8,64,256]{2,1,0:T(8,128)(2,1)S(1)}, bf16[8,64,256]{2,1,0:T(8,128)(2,1)S(1)}, bf16[8,64,256]{2,1,0:T(8,128)(2,1)S(1)}) custom-call(s32[51]{0:T(128)S(1)} %concatenate.3.facts, bf16[24,128,128]{2,1,0:T(8,128)(2,1)S(1)} %get-tuple-element.14.values, bf16[16,64,256]{2,1,0:T(8,128)(2,1)S(1)} %all_to_all.16.own, ...), custom_call_target="tpu_custom_call" | custom-call | tf_op jit(solution)/shard_map/pallas_call | solution.py:168
  109.1 1.9 %collective-permute-start.3 = (bf16[8,64,256]{2,1,0:T(8,128)(2,1)S(1)}, bf16[8,64,256]{2,1,0:T(8,128)(2,1)S(1)}, u32[]{:S(2)}, u32[]{:S(2)}) collective-permute-start(bf16[8,64,256]{2,1,0:T(8,128)(2,1)S(1)} %get-tuple-element.19), channel_id=1, source_target_pairs={{0,64},{32,992},{64,128},{96,32},{128,192},{160,96},{192,256},{224... | collective-permute-start | bytes 786440 | tf_op jit(solution)/shard_map/ppermute | solution.py:175
  111.0 3.6 %collective-permute-start.4 = (bf16[8,64,256]{2,1,0:T(8,128)(2,1)S(1)}, bf16[8,64,256]{2,1,0:T(8,128)(2,1)S(1)}, u32[]{:S(2)}, u32[]{:S(2)}) collective-permute-start(bf16[8,64,256]{2,1,0:T(8,128)(2,1)S(1)} %get-tuple-element.20), channel_id=1, source_target_pairs={{0,32},{32,64},{64,96},{96,128},{128,160},{160,192},{192,224},{224... | collective-permute-start | bytes 786440 | tf_op jit(solution)/shard_map/ppermute | solution.py:176
  114.6 2.9 %collective-permute-start.5 = (bf16[8,64,256]{2,1,0:T(8,128)(2,1)S(1)}, bf16[8,64,256]{2,1,0:T(8,128)(2,1)S(1)}, u32[]{:S(2)}, u32[]{:S(2)}) collective-permute-start(bf16[8,64,256]{2,1,0:T(8,128)(2,1)S(1)} %get-tuple-element.21), channel_id=1, source_target_pairs={{0,992},{32,0},{64,32},{96,64},{128,96},{160,128},{192,160},{224,1... | collective-permute-start | bytes 786440 | tf_op jit(solution)/shard_map/ppermute | solution.py:177
  117.5 3.9 %collective-permute-done.3 = bf16[8,64,256]{2,1,0:T(8,128)(2,1)S(1)} collective-permute-done((bf16[8,64,256]{2,1,0:T(8,128)(2,1)S(1)}, bf16[8,64,256]{2,1,0:T(8,128)(2,1)S(1)}, u32[]{:S(2)}, u32[]{:S(2)}) %collective-permute-start.3) | collective-permute-done | bytes 262176 | tf_op jit(solution)/shard_map/ppermute | solution.py:175
  121.4 5.6 %collective-permute-done.4 = bf16[8,64,256]{2,1,0:T(8,128)(2,1)S(1)} collective-permute-done((bf16[8,64,256]{2,1,0:T(8,128)(2,1)S(1)}, bf16[8,64,256]{2,1,0:T(8,128)(2,1)S(1)}, u32[]{:S(2)}, u32[]{:S(2)}) %collective-permute-start.4) | collective-permute-done | bytes 262176 | tf_op jit(solution)/shard_map/ppermute | solution.py:176
  127.0 0.0 collective-permute-done.5
  127.0 0.1 add_convert_fusion.1
  127.1 0.0 copy-start.1
  127.1 49.1 %all_to_all.17.parts = bf16[8,64,256]{2,1,0:T(8,128)(2,1)S(1)} all-to-all(bf16[8,64,256]{2,1,0:T(8,128)(2,1)S(1)} %add_convert_fusion.1), channel_id=1, replica_groups={{0,128,256,384,512,640,768,896},{32,160,288,416,544,672,800,928},{64,19..., dimensions={0} | all-to-all | bytes 524288 | tf_op jit(solution)/shard_map/all_to_all | solution.py:179
  176.2 0.0 copy-done.1
  176.2 0.8 shard_map.95
Async XLA Ops:
  45.2 9.9 %collective-permute-start = (bf16[16,64,256]{2,1,0:T(8,128)(2,1)S(1)}, bf16[16,64,256]{2,1,0:T(8,128)(2,1)S(1)}, u32[]{:S(2)}, u32[]{:S(2)}) collective-permute-start(bf16[16,64,256]{2,1,0:T(8,128)(2,1)S(1)} %bitcast.10), channel_id=1, source_target_pairs={{0,32},{32,0},{64,96},{96,64},{128,160},{160,128},{192,224},{224,1... | collective-permute-start | bytes 1572872 | tf_op jit(solution)/shard_map/ppermute | solution.py:148
  47.8 0.7 copy-start.4
  48.5 0.7 copy-start.3
  49.2 1.1 copy-start
  50.4 0.7 copy-start.5
  50.4 0.7 copy-start.6
  57.4 12.1 %collective-permute-start.1 = (f32[16,64,256]{2,1,0:T(8,128)S(1)}, f32[16,64,256]{2,1,0:T(8,128)S(1)}, u32[]{:S(2)}, u32[]{:S(2)}) collective-permute-start(f32[16,64,256]{2,1,0:T(8,128)S(1)} %get-tuple-element.16), channel_id=1, source_target_pairs={{0,1},{1,0},{2,3},{3,2},{4,5},{5,4},{6,7},{7,6},{8,9},{9,8},{10,11... | collective-permute-start | bytes 3145736 | tf_op jit(solution)/shard_map/ppermute | solution.py:159
  69.7 17.5 %copy-start.2 = (bf16[256,256]{1,0:T(8,128)(2,1)S(1)}, bf16[256,256]{1,0:T(8,128)(2,1)}, u32[]{:S(2)}) copy-start(bf16[256,256]{1,0:T(8,128)(2,1)} %weight.2) | copy-start | bytes 393220
  100.9 5.8 %collective-permute-start.2 = (bf16[16,64,256]{2,1,0:T(8,128)(2,1)S(1)}, bf16[16,64,256]{2,1,0:T(8,128)(2,1)S(1)}, u32[]{:S(2)}, u32[]{:S(2)}) collective-permute-start(bf16[16,64,256]{2,1,0:T(8,128)(2,1)S(1)} %all_to_all.16.own), channel_id=1, source_target_pairs={{0,1},{1,0},{2,3},{3,2},{4,5},{5,4},{6,7},{7,6},{8,9},{9,8},{10,11... | collective-permute-start | bytes 1572872 | tf_op jit(solution)/shard_map/ppermute | solution.py:166
  109.1 12.3 %collective-permute-start.3 = (bf16[8,64,256]{2,1,0:T(8,128)(2,1)S(1)}, bf16[8,64,256]{2,1,0:T(8,128)(2,1)S(1)}, u32[]{:S(2)}, u32[]{:S(2)}) collective-permute-start(bf16[8,64,256]{2,1,0:T(8,128)(2,1)S(1)} %get-tuple-element.19), channel_id=1, source_target_pairs={{0,64},{32,992},{64,128},{96,32},{128,192},{160,96},{192,256},{224... | collective-permute-start | bytes 786440 | tf_op jit(solution)/shard_map/ppermute | solution.py:175
  111.0 16.0 %collective-permute-start.4 = (bf16[8,64,256]{2,1,0:T(8,128)(2,1)S(1)}, bf16[8,64,256]{2,1,0:T(8,128)(2,1)S(1)}, u32[]{:S(2)}, u32[]{:S(2)}) collective-permute-start(bf16[8,64,256]{2,1,0:T(8,128)(2,1)S(1)} %get-tuple-element.20), channel_id=1, source_target_pairs={{0,32},{32,64},{64,96},{96,128},{128,160},{160,192},{192,224},{224... | collective-permute-start | bytes 786440 | tf_op jit(solution)/shard_map/ppermute | solution.py:176
  114.6 12.3 %collective-permute-start.5 = (bf16[8,64,256]{2,1,0:T(8,128)(2,1)S(1)}, bf16[8,64,256]{2,1,0:T(8,128)(2,1)S(1)}, u32[]{:S(2)}, u32[]{:S(2)}) collective-permute-start(bf16[8,64,256]{2,1,0:T(8,128)(2,1)S(1)} %get-tuple-element.21), channel_id=1, source_target_pairs={{0,992},{32,0},{64,32},{96,64},{128,96},{160,128},{192,160},{224,1... | collective-permute-start | bytes 786440 | tf_op jit(solution)/shard_map/ppermute | solution.py:177
  127.1 49.1 %copy-start.1 = (bf16[256,256]{1,0:T(8,128)(2,1)S(1)}, bf16[256,256]{1,0:T(8,128)(2,1)}, u32[]{:S(2)}) copy-start(bf16[256,256]{1,0:T(8,128)(2,1)} %weight.3) | copy-start | bytes 393220

commit v3 on v2

--- a/solution.py
+++ b/solution.py
@@ -75,7 +75,7 @@
     chips, half = keep.shape[:2]
     core = lax.rem(facts[PLACE_COL], 2)
     keep[...] = acc[:chips, pl.ds(pl.multiple_of(core * half, half), half), :]
-    send[...] = acc[:chips, pl.ds(pl.multiple_of((1 - core) * half, half), half), :]
+    send[...] = acc[:chips, pl.ds(pl.multiple_of((1 - core) * half, half), half), :].astype(BF16)
 
 
 def second_kernel(facts, values, own, other, keep, two, up, down, panel, acc):
@@ -92,8 +92,12 @@
 
 
 def dense_kernel(layer, parts, weight, bias, out):
-    total = jnp.sum(parts[...].astype(F32), axis=0).astype(BF16)
-    result = jnp.dot(total, weight[...], preferred_element_type=F32) + bias[...]
+    total = jnp.sum(parts[...].astype(F32), axis=0)
+    high = total.astype(BF16)
+    low = (total - high.astype(F32)).astype(BF16)
+    result = jnp.dot(low, weight[...], preferred_element_type=F32)
+    result += jnp.dot(high, weight[...], preferred_element_type=F32)
+    result += bias[...]
     if layer == 0:
         result = jnp.maximum(result, 0.0)
     result = result.astype(BF16)
@@ -153,10 +157,10 @@
         same, values, b_first.reshape(bias_shape), b_second.reshape(bias_shape)
     )
     keep, send = call(
-        first_kernel, (shape(piece, F32), shape(piece, F32)), [SMEM] + [VMEM] * 3, scratch
+        first_kernel, (shape(piece, F32), shape(piece, BF16)), [SMEM] + [VMEM] * 3, scratch
     )(facts, values, same, other)
 
-    summed = (keep + lax.ppermute(send, COL, swap(cols))).astype(BF16)
+    summed = (keep + lax.ppermute(send, COL, swap(cols)).astype(F32)).astype(BF16)
     terms = lax.all_to_all(summed, COL, 0, 0, axis_index_groups=strided(cols, 2))
     copies = call(functools.partial(dense_kernel, 0), shape(piece, BF16), [VMEM] * 3)(
         terms, w_first, bias_first

time: 177 us -> 177 us (level)
  the two profiles are of different devices: /device:TPU:1 before, /device:TPU:6 now
where the time goes in v3:
time: 177 us; the launch traced here: 175 us
  blocking collectives  133 us (75%)
  waiting for transfers between devices  16.8 us (9%)
  starting transfers between devices  15.4 us (9%)
  Pallas kernels  5.8 us (3%)
  local copies, waits for them, and re-layouts  2.55 us (1%)
    all_to_all x1, blocking collectives, per_device(): lax.all_to_all(summed, ROW, 0, 0, axis_index_groups=strided(rows, 4))  51.7 us
    all_gather x1, blocking collectives, per_device(): same = lax.all_gather(features, ROW, axis_index_groups=strided(rows, 2))  51.2 us
    all_to_all x1, blocking collectives, per_device(): lax.all_to_all(summed, COL, 0, 0, axis_index_groups=strided(cols, 2))  16.6 us
    all_to_all x1, blocking collectives, per_device(): mine = lax.all_to_all(copies, COL, 0, 0, axis_index_groups=strided(cols, 2))  14 us
    ppermute x1, waiting for transfers between devices, per_device(): other = lax.ppermute(same, ROW, swap(rows))  5.16 us
    ppermute x1, starting transfers between devices, per_device(): up = lax.ppermute(up, ROW, shift(rows, 1))  4.45 us
    ppermute x1, waiting for transfers between devices, per_device(): two = lax.ppermute(two, ROW, hop_two(rows))  4.29 us
    ppermute x1, waiting for transfers between devices, per_device(): up = lax.ppermute(up, ROW, shift(rows, 1))  3.61 us
  transfers between devices with their start and end apart: 6, of which 5 were waited for; matrix products, arithmetic and copies ran while one was open for 0% of the time, Pallas kernels for 0%

profile of v3, /device:TPU:6, one launch (start us, length us, event | category | flops | bytes accessed | tf_op | source)
XLA Modules:
  0.0 175.1 jit_solution(2486124897332421137)
XLA Ops:
  0.0 51.2 %all-gather = bf16[1024,256]{1,0:T(8,128)(2,1)S(1)} all-gather(bf16[64,256]{1,0:T(8,128)(2,1)} %param.9), channel_id=2, replica_groups={{0,64,128,192,256,320,384,448,512,576,640,704,768,832,896,960},{32,96,1..., dimensions={0}, use_global_device_ids=true | all-gather | bytes 557056 | tf_op jit(solution)/shard_map/all_gather | solution.py:151
  51.2 2.6 %collective-permute-start = (bf16[16,64,256]{2,1,0:T(8,128)(2,1)S(1)}, bf16[16,64,256]{2,1,0:T(8,128)(2,1)S(1)}, u32[]{:S(2)}, u32[]{:S(2)}) collective-permute-start(bf16[16,64,256]{2,1,0:T(8,128)(2,1)S(1)} %bitcast.10), channel_id=1, source_target_pairs={{0,32},{32,0},{64,96},{96,64},{128,160},{160,128},{192,224},{224,1... | collective-permute-start | bytes 1572872 | tf_op jit(solution)/shard_map/ppermute | solution.py:152
  53.8 0.0 copy-start.4
  54.5 0.0 copy-start.3
  54.5 0.0 copy-done.4
  54.5 0.7 copy-done.3
  55.1 0.0 copy-start
  55.1 1.1 copy-done
  56.3 0.1 shard_map.91
  56.3 0.0 copy-start.5
  56.3 0.0 copy-start.6
  56.4 0.6 copy-done.5
  57.0 0.0 copy-done.6
  57.0 0.1 concatenate.3.facts
  57.1 5.2 %collective-permute-done.other = bf16[16,64,256]{2,1,0:T(8,128)(2,1)S(1)} collective-permute-done((bf16[16,64,256]{2,1,0:T(8,128)(2,1)S(1)}, bf16[16,64,256]{2,1,0:T(8,128)(2,1)S(1)}, u32[]{:S(2)}, u32[]{:S(2)}) %collective-permute-start) | collective-permute-done | bytes 524320 | tf_op jit(solution)/shard_map/ppermute | solution.py:152
  62.2 2.3 %shard_map.92 = (f32[16,64,256]{2,1,0:T(8,128)S(1)}, bf16[16,64,256]{2,1,0:T(8,128)(2,1)S(1)}) custom-call(s32[51]{0:T(128)S(1)} %concatenate.3.facts, bf16[24,128,128]{2,1,0:T(8,128)(2,1)S(1)} %get-tuple-element.14.values, bf16[16,64,256]{2,1,0:T(8,128)(2,1)S(1)} %bitcast.12, bf16[16,64,256]{2,1,0:T(8,128)(2,1)S(1)} %collective-permute-done.other), custom_call_target="tpu_custom_call" | custom-call | tf_op jit(solution)/shard_map/pallas_call | solution.py:159
  64.5 1.9 %collective-permute-start.1 = (bf16[16,64,256]{2,1,0:T(8,128)(2,1)S(1)}, bf16[16,64,256]{2,1,0:T(8,128)(2,1)S(1)}, u32[]{:S(2)}, u32[]{:S(2)}) collective-permute-start(bf16[16,64,256]{2,1,0:T(8,128)(2,1)S(1)} %get-tuple-element.16), channel_id=1, source_target_pairs={{0,1},{1,0},{2,3},{3,2},{4,5},{5,4},{6,7},{7,6},{8,9},{9,8},{10,11... | collective-permute-start | bytes 1572872 | tf_op jit(solution)/shard_map/ppermute | solution.py:163
  66.4 1.9 %collective-permute-done.1 = bf16[16,64,256]{2,1,0:T(8,128)(2,1)S(1)} collective-permute-done((bf16[16,64,256]{2,1,0:T(8,128)(2,1)S(1)}, bf16[16,64,256]{2,1,0:T(8,128)(2,1)S(1)}, u32[]{:S(2)}, u32[]{:S(2)}) %collective-permute-start.1) | collective-permute-done | bytes 524320 | tf_op jit(solution)/shard_map/ppermute | solution.py:163
  68.3 0.1 add_convert_fusion
  68.5 0.0 copy-start.2
  68.5 16.6 %all_to_all.15.parts = bf16[16,64,256]{2,1,0:T(8,128)(2,1)S(1)} all-to-all(bf16[16,64,256]{2,1,0:T(8,128)(2,1)S(1)} %add_convert_fusion), channel_id=1, replica_groups={{0,2,4,6,8,10,12,14,16,18,20,22,24,26,28,30},{1,3,5,7,9,11,13,15,17,19,..., dimensions={0} | all-to-all | bytes 1048576 | tf_op jit(solution)/shard_map/all_to_all | solution.py:164
  85.0 0.0 copy-done.2
  85.0 0.2 shard_map.93
  85.3 14.0 %all_to_all.16.own = bf16[16,64,256]{2,1,0:T(8,128)(2,1)S(1)} all-to-all(bf16[16,64,256]{2,1,0:T(8,128)(2,1)S(1)} %shard_map.93), channel_id=1, replica_groups={{0,2,4,6,8,10,12,14,16,18,20,22,24,26,28,30},{1,3,5,7,9,11,13,15,17,19,..., dimensions={0} | all-to-all | bytes 1048576 | tf_op jit(solution)/shard_map/all_to_all | solution.py:169
  99.3 1.9 %collective-permute-start.2 = (bf16[16,64,256]{2,1,0:T(8,128)(2,1)S(1)}, bf16[16,64,256]{2,1,0:T(8,128)(2,1)S(1)}, u32[]{:S(2)}, u32[]{:S(2)}) collective-permute-start(bf16[16,64,256]{2,1,0:T(8,128)(2,1)S(1)} %all_to_all.16.own), channel_id=1, source_target_pairs={{0,1},{1,0},{2,3},{3,2},{4,5},{5,4},{6,7},{7,6},{8,9},{9,8},{10,11... | collective-permute-start | bytes 1572872 | tf_op jit(solution)/shard_map/ppermute | solution.py:170
  101.2 1.9 %collective-permute-done.2.other = bf16[16,64,256]{2,1,0:T(8,128)(2,1)S(1)} collective-permute-done((bf16[16,64,256]{2,1,0:T(8,128)(2,1)S(1)}, bf16[16,64,256]{2,1,0:T(8,128)(2,1)S(1)}, u32[]{:S(2)}, u32[]{:S(2)}) %collective-permute-start.2) | collective-permute-done | bytes 524320 | tf_op jit(solution)/shard_map/ppermute | solution.py:170
  103.1 2.5 %shard_map.94 = (f32[8,64,256]{2,1,0:T(8,128)S(1)}, bf16[8,64,256]{2,1,0:T(8,128)(2,1)S(1)}, bf16[8,64,256]{2,1,0:T(8,128)(2,1)S(1)}, bf16[8,64,256]{2,1,0:T(8,128)(2,1)S(1)}) custom-call(s32[51]{0:T(128)S(1)} %concatenate.3.facts, bf16[24,128,128]{2,1,0:T(8,128)(2,1)S(1)} %get-tuple-element.14.values, bf16[16,64,256]{2,1,0:T(8,128)(2,1)S(1)} %all_to_all.16.own, ...), custom_call_target="tpu_custom_call" | custom-call | tf_op jit(solution)/shard_map/pallas_call | solution.py:172
  105.5 1.9 %collective-permute-start.3 = (bf16[8,64,256]{2,1,0:T(8,128)(2,1)S(1)}, bf16[8,64,256]{2,1,0:T(8,128)(2,1)S(1)}, u32[]{:S(2)}, u32[]{:S(2)}) collective-permute-start(bf16[8,64,256]{2,1,0:T(8,128)(2,1)S(1)} %get-tuple-element.19), channel_id=1, source_target_pairs={{0,64},{32,992},{64,128},{96,32},{128,192},{160,96},{192,256},{224... | collective-permute-start | bytes 786440 | tf_op jit(solution)/shard_map/ppermute | solution.py:179
  107.5 4.5 %collective-permute-start.4 = (bf16[8,64,256]{2,1,0:T(8,128)(2,1)S(1)}, bf16[8,64,256]{2,1,0:T(8,128)(2,1)S(1)}, u32[]{:S(2)}, u32[]{:S(2)}) collective-permute-start(bf16[8,64,256]{2,1,0:T(8,128)(2,1)S(1)} %get-tuple-element.20), channel_id=1, source_target_pairs={{0,32},{32,64},{64,96},{96,128},{128,160},{160,192},{192,224},{224... | collective-permute-start | bytes 786440 | tf_op jit(solution)/shard_map/ppermute | solution.py:180
  111.9 2.6 %collective-permute-start.5 = (bf16[8,64,256]{2,1,0:T(8,128)(2,1)S(1)}, bf16[8,64,256]{2,1,0:T(8,128)(2,1)S(1)}, u32[]{:S(2)}, u32[]{:S(2)}) collective-permute-start(bf16[8,64,256]{2,1,0:T(8,128)(2,1)S(1)} %get-tuple-element.21), channel_id=1, source_target_pairs={{0,992},{32,0},{64,32},{96,64},{128,96},{160,128},{192,160},{224,1... | collective-permute-start | bytes 786440 | tf_op jit(solution)/shard_map/ppermute | solution.py:181
  114.5 4.3 %collective-permute-done.3 = bf16[8,64,256]{2,1,0:T(8,128)(2,1)S(1)} collective-permute-done((bf16[8,64,256]{2,1,0:T(8,128)(2,1)S(1)}, bf16[8,64,256]{2,1,0:T(8,128)(2,1)S(1)}, u32[]{:S(2)}, u32[]{:S(2)}) %collective-permute-start.3) | collective-permute-done | bytes 262176 | tf_op jit(solution)/shard_map/ppermute | solution.py:179
  118.8 3.6 %collective-permute-done.4 = bf16[8,64,256]{2,1,0:T(8,128)(2,1)S(1)} collective-permute-done((bf16[8,64,256]{2,1,0:T(8,128)(2,1)S(1)}, bf16[8,64,256]{2,1,0:T(8,128)(2,1)S(1)}, u32[]{:S(2)}, u32[]{:S(2)}) %collective-permute-start.4) | collective-permute-done | bytes 262176 | tf_op jit(solution)/shard_map/ppermute | solution.py:180
  122.4 0.0 collective-permute-done.5
  122.4 0.1 add_convert_fusion.1
  122.6 0.0 copy-start.1
  122.6 51.7 %all_to_all.17.parts = bf16[8,64,256]{2,1,0:T(8,128)(2,1)S(1)} all-to-all(bf16[8,64,256]{2,1,0:T(8,128)(2,1)S(1)} %add_convert_fusion.1), channel_id=1, replica_groups={{0,128,256,384,512,640,768,896},{32,160,288,416,544,672,800,928},{64,19..., dimensions={0} | all-to-all | bytes 524288 | tf_op jit(solution)/shard_map/all_to_all | solution.py:183
  174.3 0.0 copy-done.1
  174.3 0.8 shard_map.95
Async XLA Ops:
  51.2 11.1 %collective-permute-start = (bf16[16,64,256]{2,1,0:T(8,128)(2,1)S(1)}, bf16[16,64,256]{2,1,0:T(8,128)(2,1)S(1)}, u32[]{:S(2)}, u32[]{:S(2)}) collective-permute-start(bf16[16,64,256]{2,1,0:T(8,128)(2,1)S(1)} %bitcast.10), channel_id=1, source_target_pairs={{0,32},{32,0},{64,96},{96,64},{128,160},{160,128},{192,224},{224,1... | collective-permute-start | bytes 1572872 | tf_op jit(solution)/shard_map/ppermute | solution.py:152
  53.8 0.7 copy-start.4
  54.5 0.7 copy-start.3
  55.1 1.1 copy-start
  56.3 0.7 copy-start.5
  56.3 0.7 copy-start.6
  64.5 3.8 %collective-permute-start.1 = (bf16[16,64,256]{2,1,0:T(8,128)(2,1)S(1)}, bf16[16,64,256]{2,1,0:T(8,128)(2,1)S(1)}, u32[]{:S(2)}, u32[]{:S(2)}) collective-permute-start(bf16[16,64,256]{2,1,0:T(8,128)(2,1)S(1)} %get-tuple-element.16), channel_id=1, source_target_pairs={{0,1},{1,0},{2,3},{3,2},{4,5},{5,4},{6,7},{7,6},{8,9},{9,8},{10,11... | collective-permute-start | bytes 1572872 | tf_op jit(solution)/shard_map/ppermute | solution.py:163
  68.5 16.6 %copy-start.2 = (bf16[256,256]{1,0:T(8,128)(2,1)S(1)}, bf16[256,256]{1,0:T(8,128)(2,1)}, u32[]{:S(2)}) copy-start(bf16[256,256]{1,0:T(8,128)(2,1)} %weight.2) | copy-start | bytes 393220
  99.3 3.8 %collective-permute-start.2 = (bf16[16,64,256]{2,1,0:T(8,128)(2,1)S(1)}, bf16[16,64,256]{2,1,0:T(8,128)(2,1)S(1)}, u32[]{:S(2)}, u32[]{:S(2)}) collective-permute-start(bf16[16,64,256]{2,1,0:T(8,128)(2,1)S(1)} %all_to_all.16.own), channel_id=1, source_target_pairs={{0,1},{1,0},{2,3},{3,2},{4,5},{5,4},{6,7},{7,6},{8,9},{9,8},{10,11... | collective-permute-start | bytes 1572872 | tf_op jit(solution)/shard_map/ppermute | solution.py:170
  105.5 13.3 %collective-permute-start.3 = (bf16[8,64,256]{2,1,0:T(8,128)(2,1)S(1)}, bf16[8,64,256]{2,1,0:T(8,128)(2,1)S(1)}, u32[]{:S(2)}, u32[]{:S(2)}) collective-permute-start(bf16[8,64,256]{2,1,0:T(8,128)(2,1)S(1)} %get-tuple-element.19), channel_id=1, source_target_pairs={{0,64},{32,992},{64,128},{96,32},{128,192},{160,96},{192,256},{224... | collective-permute-start | bytes 786440 | tf_op jit(solution)/shard_map/ppermute | solution.py:179
  107.5 15.0 %collective-permute-start.4 = (bf16[8,64,256]{2,1,0:T(8,128)(2,1)S(1)}, bf16[8,64,256]{2,1,0:T(8,128)(2,1)S(1)}, u32[]{:S(2)}, u32[]{:S(2)}) collective-permute-start(bf16[8,64,256]{2,1,0:T(8,128)(2,1)S(1)} %get-tuple-element.20), channel_id=1, source_target_pairs={{0,32},{32,64},{64,96},{96,128},{128,160},{160,192},{192,224},{224... | collective-permute-start | bytes 786440 | tf_op jit(solution)/shard_map/ppermute | solution.py:180
  111.9 10.5 %collective-permute-start.5 = (bf16[8,64,256]{2,1,0:T(8,128)(2,1)S(1)}, bf16[8,64,256]{2,1,0:T(8,128)(2,1)S(1)}, u32[]{:S(2)}, u32[]{:S(2)}) collective-permute-start(bf16[8,64,256]{2,1,0:T(8,128)(2,1)S(1)} %get-tuple-element.21), channel_id=1, source_target_pairs={{0,992},{32,0},{64,32},{96,64},{128,96},{160,128},{192,160},{224,1... | collective-permute-start | bytes 786440 | tf_op jit(solution)/shard_map/ppermute | solution.py:181
  122.6 51.7 %copy-start.1 = (bf16[256,256]{1,0:T(8,128)(2,1)S(1)}, bf16[256,256]{1,0:T(8,128)(2,1)}, u32[]{:S(2)}) copy-start(bf16[256,256]{1,0:T(8,128)(2,1)} %weight.3) | copy-start | bytes 393220

commit v4 on v3

--- a/solution.py
+++ b/solution.py
@@ -25,7 +25,12 @@
 
 
 def hop_two(size):
-    return [(i, (i + (2 if i % 2 == 0 else -2)) % size) for i in range(size)]
+    return [(i, (i + (-2 if i % 2 == 0 else 2)) % size) for i in range(size)]
+
+
+def quartets(size):
+    quads = size // 4
+    return [[4 * j + (g if j < quads // 2 else g ^ 1) for j in range(quads)] for g in range(4)]
 
 
 def swap(size):
@@ -84,11 +89,16 @@
     slots = values.shape[0]
     add_products(panel, acc, facts, FIRST, FIRST + slots, values, True)
     quads, half = keep.shape[:2]
-    for ref, by in ((two, 2), (up, 1), (down, 3), (keep, 0)):
-        r = lax.rem(facts[PLACE_ROW] + by, 4)
-        offset = pl.multiple_of(lax.rem(r, 2) * half, half)
-        for k in range(quads):
-            ref[k] = acc[2 * k + r // 2, pl.ds(offset, half), :].astype(ref.dtype)
+    rows = 4 * quads
+    z = facts[PLACE_ROW]
+    odd = lax.rem(z, 2)
+    for ref, to in ((two, z + 4 * odd - 2), (up, z + 1), (down, z - 1), (keep, z)):
+        to = lax.rem(to + rows, rows)
+        g = lax.rem(to, 4) ^ (to >= rows // 2).astype(jnp.int32)
+        for j in range(quads):
+            side = lax.rem(g + (0 if j < quads // 2 else 1), 2)
+            offset = pl.multiple_of(side * half, half)
+            ref[j] = acc[2 * j + g // 2, pl.ds(offset, half), :].astype(ref.dtype)
 
 
 def dense_kernel(layer, parts, weight, bias, out):
@@ -180,7 +190,7 @@
     up = lax.ppermute(up, ROW, shift(rows, 1))
     down = lax.ppermute(down, ROW, shift(rows, -1))
     summed = (keep + two.astype(F32) + up.astype(F32) + down.astype(F32)).astype(BF16)
-    terms = lax.all_to_all(summed, ROW, 0, 0, axis_index_groups=strided(rows, 4))
+    terms = lax.all_to_all(summed, ROW, 0, 0, axis_index_groups=quartets(rows))
     return call(functools.partial(dense_kernel, 1), shape((own_rows, width), BF16), [VMEM] * 3)(
         terms, w_second, bias_second
     )

time: 177 us -> 178 us (level)
  Pallas kernels: 5.8 us -> 3.33 us
  blocking collectives: 133 us -> 135 us
    ppermute x1, waiting for transfers between devices: 4.29 us -> 1.31 us  [per_device(): two = lax.ppermute(two, ROW, hop_two(rows))]
    ppermute x1, starting transfers between devices: 2.6 us -> 4.83 us  [per_device(): down = lax.ppermute(down, ROW, shift(rows, -1))]
    ppermute x1, starting transfers between devices: 4.45 us -> 2.22 us  [per_device(): up = lax.ppermute(up, ROW, shift(rows, 1))]
  transfers between devices with their start and end apart: 6 -> 6, of which waited for: 5 -> 6; matrix products, arithmetic and copies ran while one was open for 0% -> 0% of each run, Pallas kernels for 0% -> 0%
where the time goes in v4:
time: 178 us; the launch traced here: 175 us
  blocking collectives  135 us (76%)
  starting transfers between devices  17.1 us (10%)
  waiting for transfers between devices  15.7 us (9%)
  Pallas kernels  3.33 us (2%)
  local copies, waits for them, and re-layouts  2.55 us (1%)
    all_to_all x1, blocking collectives, per_device(): terms = lax.all_to_all(summed, ROW, 0, 0, axis_index_groups=quartets(rows))  53.1 us
    all_gather x1, blocking collectives, per_device(): same = lax.all_gather(features, ROW, axis_index_groups=strided(rows, 2))  51.2 us
    all_to_all x1, blocking collectives, per_device(): lax.all_to_all(summed, COL, 0, 0, axis_index_groups=strided(cols, 2))  17.2 us
    all_to_all x1, blocking collectives, per_device(): mine = lax.all_to_all(copies, COL, 0, 0, axis_index_groups=strided(cols, 2))  14 us
    ppermute x1, waiting for transfers between devices, per_device(): other = lax.ppermute(same, ROW, swap(rows))  5.16 us
    ppermute x1, starting transfers between devices, per_device(): down = lax.ppermute(down, ROW, shift(rows, -1))  4.83 us
    ppermute x1, waiting for transfers between devices, per_device(): up = lax.ppermute(up, ROW, shift(rows, 1))  4.71 us
    ppermute x1, starting transfers between devices, per_device(): two = lax.ppermute(two, ROW, hop_two(rows))  3.65 us
  transfers between devices with their start and end apart: 6, of which 6 were waited for; matrix products, arithmetic and copies ran while one was open for 0% of the time, Pallas kernels for 0%

profile of v4, /device:TPU:6, one launch (start us, length us, event | category | flops | bytes accessed | tf_op | source)
XLA Modules:
  0.0 175.3 jit_solution(5163627740518515415)
XLA Ops:
  0.0 51.2 %all-gather = bf16[1024,256]{1,0:T(8,128)(2,1)S(1)} all-gather(bf16[64,256]{1,0:T(8,128)(2,1)} %param.9), channel_id=2, replica_groups={{0,64,128,192,256,320,384,448,512,576,640,704,768,832,896,960},{32,96,1..., dimensions={0}, use_global_device_ids=true | all-gather | bytes 557056 | tf_op jit(solution)/shard_map/all_gather | solution.py:161
  51.2 2.6 %collective-permute-start = (bf16[16,64,256]{2,1,0:T(8,128)(2,1)S(1)}, bf16[16,64,256]{2,1,0:T(8,128)(2,1)S(1)}, u32[]{:S(2)}, u32[]{:S(2)}) collective-permute-start(bf16[16,64,256]{2,1,0:T(8,128)(2,1)S(1)} %bitcast.10), channel_id=1, source_target_pairs={{0,32},{32,0},{64,96},{96,64},{128,160},{160,128},{192,224},{224,1... | collective-permute-start | bytes 1572872 | tf_op jit(solution)/shard_map/ppermute | solution.py:162
  53.8 0.0 copy-start.4
  54.5 0.0 copy-start.3
  54.5 0.0 copy-done.4
  54.5 0.7 copy-done.3
  55.1 0.0 copy-start
  55.1 1.1 copy-done
  56.3 0.1 shard_map.91
  56.3 0.0 copy-start.5
  56.3 0.0 copy-start.6
  56.4 0.6 copy-done.5
  57.0 0.0 copy-done.6
  57.0 0.1 concatenate.3.facts
  57.1 5.2 %collective-permute-done.other = bf16[16,64,256]{2,1,0:T(8,128)(2,1)S(1)} collective-permute-done((bf16[16,64,256]{2,1,0:T(8,128)(2,1)S(1)}, bf16[16,64,256]{2,1,0:T(8,128)(2,1)S(1)}, u32[]{:S(2)}, u32[]{:S(2)}) %collective-permute-start) | collective-permute-done | bytes 524320 | tf_op jit(solution)/shard_map/ppermute | solution.py:162
  62.2 1.1 shard_map.92
  63.4 1.9 %collective-permute-start.1 = (bf16[16,64,256]{2,1,0:T(8,128)(2,1)S(1)}, bf16[16,64,256]{2,1,0:T(8,128)(2,1)S(1)}, u32[]{:S(2)}, u32[]{:S(2)}) collective-permute-start(bf16[16,64,256]{2,1,0:T(8,128)(2,1)S(1)} %get-tuple-element.16), channel_id=1, source_target_pairs={{0,1},{1,0},{2,3},{3,2},{4,5},{5,4},{6,7},{7,6},{8,9},{9,8},{10,11... | collective-permute-start | bytes 1572872 | tf_op jit(solution)/shard_map/ppermute | solution.py:173
  65.3 1.9 %collective-permute-done.1 = bf16[16,64,256]{2,1,0:T(8,128)(2,1)S(1)} collective-permute-done((bf16[16,64,256]{2,1,0:T(8,128)(2,1)S(1)}, bf16[16,64,256]{2,1,0:T(8,128)(2,1)S(1)}, u32[]{:S(2)}, u32[]{:S(2)}) %collective-permute-start.1) | collective-permute-done | bytes 524320 | tf_op jit(solution)/shard_map/ppermute | solution.py:173
  67.2 0.1 add_convert_fusion
  67.3 0.0 copy-start.2
  67.3 17.2 %all_to_all.15.parts = bf16[16,64,256]{2,1,0:T(8,128)(2,1)S(1)} all-to-all(bf16[16,64,256]{2,1,0:T(8,128)(2,1)S(1)} %add_convert_fusion), channel_id=1, replica_groups={{0,2,4,6,8,10,12,14,16,18,20,22,24,26,28,30},{1,3,5,7,9,11,13,15,17,19,..., dimensions={0} | all-to-all | bytes 1048576 | tf_op jit(solution)/shard_map/all_to_all | solution.py:174
  84.6 0.0 copy-done.2
  84.6 0.2 shard_map.93
  84.8 14.0 %all_to_all.16.own = bf16[16,64,256]{2,1,0:T(8,128)(2,1)S(1)} all-to-all(bf16[16,64,256]{2,1,0:T(8,128)(2,1)S(1)} %shard_map.93), channel_id=1, replica_groups={{0,2,4,6,8,10,12,14,16,18,20,22,24,26,28,30},{1,3,5,7,9,11,13,15,17,19,..., dimensions={0} | all-to-all | bytes 1048576 | tf_op jit(solution)/shard_map/all_to_all | solution.py:179
  98.8 1.9 %collective-permute-start.2 = (bf16[16,64,256]{2,1,0:T(8,128)(2,1)S(1)}, bf16[16,64,256]{2,1,0:T(8,128)(2,1)S(1)}, u32[]{:S(2)}, u32[]{:S(2)}) collective-permute-start(bf16[16,64,256]{2,1,0:T(8,128)(2,1)S(1)} %all_to_all.16.own), channel_id=1, source_target_pairs={{0,1},{1,0},{2,3},{3,2},{4,5},{5,4},{6,7},{7,6},{8,9},{9,8},{10,11... | collective-permute-start | bytes 1572872 | tf_op jit(solution)/shard_map/ppermute | solution.py:180
  100.7 1.9 %collective-permute-done.2.other = bf16[16,64,256]{2,1,0:T(8,128)(2,1)S(1)} collective-permute-done((bf16[16,64,256]{2,1,0:T(8,128)(2,1)S(1)}, bf16[16,64,256]{2,1,0:T(8,128)(2,1)S(1)}, u32[]{:S(2)}, u32[]{:S(2)}) %collective-permute-start.2) | collective-permute-done | bytes 524320 | tf_op jit(solution)/shard_map/ppermute | solution.py:180
  102.6 1.1 shard_map.94
  103.7 3.6 %collective-permute-start.3 = (bf16[8,64,256]{2,1,0:T(8,128)(2,1)S(1)}, bf16[8,64,256]{2,1,0:T(8,128)(2,1)S(1)}, u32[]{:S(2)}, u32[]{:S(2)}) collective-permute-start(bf16[8,64,256]{2,1,0:T(8,128)(2,1)S(1)} %get-tuple-element.19), channel_id=1, source_target_pairs={{0,960},{32,96},{64,0},{96,160},{128,64},{160,224},{192,128},{224,... | collective-permute-start | bytes 786440 | tf_op jit(solution)/shard_map/ppermute | solution.py:189
  107.4 2.2 %collective-permute-start.4 = (bf16[8,64,256]{2,1,0:T(8,128)(2,1)S(1)}, bf16[8,64,256]{2,1,0:T(8,128)(2,1)S(1)}, u32[]{:S(2)}, u32[]{:S(2)}) collective-permute-start(bf16[8,64,256]{2,1,0:T(8,128)(2,1)S(1)} %get-tuple-element.20), channel_id=1, source_target_pairs={{0,32},{32,64},{64,96},{96,128},{128,160},{160,192},{192,224},{224... | collective-permute-start | bytes 786440 | tf_op jit(solution)/shard_map/ppermute | solution.py:190
  109.6 4.8 %collective-permute-start.5 = (bf16[8,64,256]{2,1,0:T(8,128)(2,1)S(1)}, bf16[8,64,256]{2,1,0:T(8,128)(2,1)S(1)}, u32[]{:S(2)}, u32[]{:S(2)}) collective-permute-start(bf16[8,64,256]{2,1,0:T(8,128)(2,1)S(1)} %get-tuple-element.21), channel_id=1, source_target_pairs={{0,992},{32,0},{64,32},{96,64},{128,96},{160,128},{192,160},{224,1... | collective-permute-start | bytes 786440 | tf_op jit(solution)/shard_map/ppermute | solution.py:191
  114.5 1.3 collective-permute-done.3
  115.8 4.7 %collective-permute-done.4 = bf16[8,64,256]{2,1,0:T(8,128)(2,1)S(1)} collective-permute-done((bf16[8,64,256]{2,1,0:T(8,128)(2,1)S(1)}, bf16[8,64,256]{2,1,0:T(8,128)(2,1)S(1)}, u32[]{:S(2)}, u32[]{:S(2)}) %collective-permute-start.4) | collective-permute-done | bytes 262176 | tf_op jit(solution)/shard_map/ppermute | solution.py:190
  120.5 0.8 collective-permute-done.5
  121.3 0.1 add_convert_fusion.1
  121.4 0.0 copy-start.1
  121.4 53.1 %all_to_all.17.parts = bf16[8,64,256]{2,1,0:T(8,128)(2,1)S(1)} all-to-all(bf16[8,64,256]{2,1,0:T(8,128)(2,1)S(1)} %add_convert_fusion.1), channel_id=1, replica_groups={{0,128,256,384,544,672,800,928},{32,160,288,416,512,640,768,896},{64,19..., dimensions={0} | all-to-all | bytes 524288 | tf_op jit(solution)/shard_map/all_to_all | solution.py:193
  174.5 0.0 copy-done.1
  174.5 0.8 shard_map.95
Async XLA Ops:
  51.2 11.1 %collective-permute-start = (bf16[16,64,256]{2,1,0:T(8,128)(2,1)S(1)}, bf16[16,64,256]{2,1,0:T(8,128)(2,1)S(1)}, u32[]{:S(2)}, u32[]{:S(2)}) collective-permute-start(bf16[16,64,256]{2,1,0:T(8,128)(2,1)S(1)} %bitcast.10), channel_id=1, source_target_pairs={{0,32},{32,0},{64,96},{96,64},{128,160},{160,128},{192,224},{224,1... | collective-permute-start | bytes 1572872 | tf_op jit(solution)/shard_map/ppermute | solution.py:162
  53.8 0.7 copy-start.4
  54.5 0.7 copy-start.3
  55.1 1.1 copy-start
  56.3 0.7 copy-start.5
  56.3 0.7 copy-start.6
  63.4 3.8 %collective-permute-start.1 = (bf16[16,64,256]{2,1,0:T(8,128)(2,1)S(1)}, bf16[16,64,256]{2,1,0:T(8,128)(2,1)S(1)}, u32[]{:S(2)}, u32[]{:S(2)}) collective-permute-start(bf16[16,64,256]{2,1,0:T(8,128)(2,1)S(1)} %get-tuple-element.16), channel_id=1, source_target_pairs={{0,1},{1,0},{2,3},{3,2},{4,5},{5,4},{6,7},{7,6},{8,9},{9,8},{10,11... | collective-permute-start | bytes 1572872 | tf_op jit(solution)/shard_map/ppermute | solution.py:173
  67.3 17.3 %copy-start.2 = (bf16[256,256]{1,0:T(8,128)(2,1)S(1)}, bf16[256,256]{1,0:T(8,128)(2,1)}, u32[]{:S(2)}) copy-start(bf16[256,256]{1,0:T(8,128)(2,1)} %weight.2) | copy-start | bytes 393220
  98.8 3.8 %collective-permute-start.2 = (bf16[16,64,256]{2,1,0:T(8,128)(2,1)S(1)}, bf16[16,64,256]{2,1,0:T(8,128)(2,1)S(1)}, u32[]{:S(2)}, u32[]{:S(2)}) collective-permute-start(bf16[16,64,256]{2,1,0:T(8,128)(2,1)S(1)} %all_to_all.16.own), channel_id=1, source_target_pairs={{0,1},{1,0},{2,3},{3,2},{4,5},{5,4},{6,7},{7,6},{8,9},{9,8},{10,11... | collective-permute-start | bytes 1572872 | tf_op jit(solution)/shard_map/ppermute | solution.py:180
  103.7 12.0 %collective-permute-start.3 = (bf16[8,64,256]{2,1,0:T(8,128)(2,1)S(1)}, bf16[8,64,256]{2,1,0:T(8,128)(2,1)S(1)}, u32[]{:S(2)}, u32[]{:S(2)}) collective-permute-start(bf16[8,64,256]{2,1,0:T(8,128)(2,1)S(1)} %get-tuple-element.19), channel_id=1, source_target_pairs={{0,960},{32,96},{64,0},{96,160},{128,64},{160,224},{192,128},{224,... | collective-permute-start | bytes 786440 | tf_op jit(solution)/shard_map/ppermute | solution.py:189
  107.4 13.1 %collective-permute-start.4 = (bf16[8,64,256]{2,1,0:T(8,128)(2,1)S(1)}, bf16[8,64,256]{2,1,0:T(8,128)(2,1)S(1)}, u32[]{:S(2)}, u32[]{:S(2)}) collective-permute-start(bf16[8,64,256]{2,1,0:T(8,128)(2,1)S(1)} %get-tuple-element.20), channel_id=1, source_target_pairs={{0,32},{32,64},{64,96},{96,128},{128,160},{160,192},{192,224},{224... | collective-permute-start | bytes 786440 | tf_op jit(solution)/shard_map/ppermute | solution.py:190
  109.6 11.7 %collective-permute-start.5 = (bf16[8,64,256]{2,1,0:T(8,128)(2,1)S(1)}, bf16[8,64,256]{2,1,0:T(8,128)(2,1)S(1)}, u32[]{:S(2)}, u32[]{:S(2)}) collective-permute-start(bf16[8,64,256]{2,1,0:T(8,128)(2,1)S(1)} %get-tuple-element.21), channel_id=1, source_target_pairs={{0,992},{32,0},{64,32},{96,64},{128,96},{160,128},{192,160},{224,1... | collective-permute-start | bytes 786440 | tf_op jit(solution)/shard_map/ppermute | solution.py:191
  121.4 53.1 %copy-start.1 = (bf16[256,256]{1,0:T(8,128)(2,1)S(1)}, bf16[256,256]{1,0:T(8,128)(2,1)}, u32[]{:S(2)}) copy-start(bf16[256,256]{1,0:T(8,128)(2,1)} %weight.3) | copy-start | bytes 393220

commit v5 on v3

--- a/solution.py
+++ b/solution.py
@@ -1,5 +1,3 @@
-import functools
-
 import jax
 import jax.numpy as jnp
 from jax import lax
@@ -67,15 +65,20 @@
         target[...] = source[...]
 
 
-def first_kernel(facts, values, own, other, keep, send, panel, acc):
+def first_kernel(facts, values, own, other, out, panel, acc):
     fill_panel(panel, own, other, lax.rem(facts[PLACE_ROW], 2))
     acc[...] = jnp.zeros_like(acc)
     slots = values.shape[0]
     add_products(panel, acc, facts, FIRST + slots, FIRST, values, False)
-    chips, half = keep.shape[:2]
+    out[...] = acc[: out.shape[0]].astype(BF16)
+
+
+def split_kernel(facts, parts, keep, send, total):
+    total[...] = jnp.sum(parts[...].astype(F32), axis=0)
+    half = keep.shape[0]
     core = lax.rem(facts[PLACE_COL], 2)
-    keep[...] = acc[:chips, pl.ds(pl.multiple_of(core * half, half), half), :]
-    send[...] = acc[:chips, pl.ds(pl.multiple_of((1 - core) * half, half), half), :].astype(BF16)
+    keep[...] = total[pl.ds(pl.multiple_of(core * half, half), half), :]
+    send[...] = total[pl.ds(pl.multiple_of((1 - core) * half, half), half), :]
 
 
 def second_kernel(facts, values, own, other, keep, two, up, down, panel, acc):
@@ -91,21 +94,23 @@
             ref[k] = acc[2 * k + r // 2, pl.ds(offset, half), :].astype(ref.dtype)
 
 
-def dense_kernel(layer, parts, weight, bias, out):
-    total = jnp.sum(parts[...].astype(F32), axis=0)
+def dense(total, weight, bias):
     high = total.astype(BF16)
     low = (total - high.astype(F32)).astype(BF16)
     result = jnp.dot(low, weight[...], preferred_element_type=F32)
     result += jnp.dot(high, weight[...], preferred_element_type=F32)
-    result += bias[...]
-    if layer == 0:
-        result = jnp.maximum(result, 0.0)
-    result = result.astype(BF16)
-    if len(out.shape) == 3:
-        for k in range(out.shape[0]):
-            out[k] = result
-    else:
-        out[...] = result
+    return result + bias[...]
+
+
+def hidden_kernel(keep, received, weight, bias, out):
+    result = jnp.maximum(dense(keep[...] + received[...], weight, bias), 0.0).astype(BF16)
+    for k in range(out.shape[0]):
+        out[k] = result
+
+
+def embed_kernel(parts, weight, bias, out):
+    total = jnp.sum(parts[...].astype(F32), axis=0)
+    out[...] = dense(total, weight, bias).astype(BF16)
 
 
 def call(kernel, out_shape, in_specs, scratch=()):
@@ -156,15 +161,17 @@
     values, bias_first, bias_second = call(keep_near_kernel, near, [VMEM] * 4)(
         same, values, b_first.reshape(bias_shape), b_second.reshape(bias_shape)
     )
-    keep, send = call(
-        first_kernel, (shape(piece, F32), shape(piece, BF16)), [SMEM] + [VMEM] * 3, scratch
+    partial_first = call(
+        first_kernel, shape((chips, block, width), BF16), [SMEM] + [VMEM] * 3, scratch
     )(facts, values, same, other)
 
-    summed = (keep + lax.ppermute(send, COL, swap(cols)).astype(F32)).astype(BF16)
-    terms = lax.all_to_all(summed, COL, 0, 0, axis_index_groups=strided(cols, 2))
-    copies = call(functools.partial(dense_kernel, 0), shape(piece, BF16), [VMEM] * 3)(
-        terms, w_first, bias_first
-    )
+    terms = lax.all_to_all(partial_first, COL, 0, 0, axis_index_groups=strided(cols, 2))
+    half = shape((own_rows, width), F32)
+    keep, send = call(split_kernel, (half, half), [SMEM, VMEM], (pltpu.VMEM((block, width), F32),))(
+        facts, terms
+    )
+    received = lax.ppermute(send, COL, swap(cols))
+    copies = call(hidden_kernel, shape(piece, BF16), [VMEM] * 4)(keep, received, w_first, bias_first)
 
     mine = lax.all_to_all(copies, COL, 0, 0, axis_index_groups=strided(cols, 2))
     other = lax.ppermute(mine, COL, swap(cols))
@@ -181,7 +188,7 @@
     down = lax.ppermute(down, ROW, shift(rows, -1))
     summed = (keep + two.astype(F32) + up.astype(F32) + down.astype(F32)).astype(BF16)
     terms = lax.all_to_all(summed, ROW, 0, 0, axis_index_groups=strided(rows, 4))
-    return call(functools.partial(dense_kernel, 1), shape((own_rows, width), BF16), [VMEM] * 3)(
+    return call(embed_kernel, shape((own_rows, width), BF16), [VMEM] * 3)(
         terms, w_second, bias_second
     )
 

time: 177 us -> 179 us (1.011)
  blocking collectives: 133 us -> 137 us
  Pallas kernels: 5.8 us -> 4.01 us
    all_to_all x1, blocking collectives: 51.7 us -> 53.7 us  [per_device(): lax.all_to_all(summed, ROW, 0, 0, axis_index_groups=strided(rows, 4))]
where the time goes in v5:
time: 179 us; the launch traced here: 178 us
  blocking collectives  137 us (77%)
  starting transfers between devices  16.5 us (9%)
  waiting for transfers between devices  16.2 us (9%)
  Pallas kernels  4.01 us (2%)
  local copies, waits for them, and re-layouts  2.55 us (1%)
    all_to_all x1, blocking collectives, per_device(): lax.all_to_all(summed, ROW, 0, 0, axis_index_groups=strided(rows, 4))  53.7 us
    all_gather x1, blocking collectives, per_device(): same = lax.all_gather(features, ROW, axis_index_groups=strided(rows, 2))  51.2 us
    all_to_all x1, blocking collectives, per_device(): lax.all_to_all(partial_first, COL, 0, 0, axis_index_groups=strided(cols, 2))  17.8 us
    all_to_all x1, blocking collectives, per_device(): mine = lax.all_to_all(copies, COL, 0, 0, axis_index_groups=strided(cols, 2))  14.8 us
    ppermute x1, waiting for transfers between devices, per_device(): other = lax.ppermute(same, ROW, swap(rows))  5.16 us
    ppermute x1, starting transfers between devices, per_device(): up = lax.ppermute(up, ROW, shift(rows, 1))  4.86 us
    ppermute x1, waiting for transfers between devices, per_device(): up = lax.ppermute(up, ROW, shift(rows, 1))  4.77 us
  transfers between devices with their start and end apart: 6, of which 5 were waited for; matrix products, arithmetic and copies ran while one was open for 0% of the time, Pallas kernels for 0%

profile of v5, /device:TPU:6, one launch (start us, length us, event | category | flops | bytes accessed | tf_op | source)
XLA Modules:
  0.0 177.6 jit_solution(4094402481814262625)
XLA Ops:
  0.0 51.2 %all-gather = bf16[1024,256]{1,0:T(8,128)(2,1)S(1)} all-gather(bf16[64,256]{1,0:T(8,128)(2,1)} %param.9), channel_id=2, replica_groups={{0,64,128,192,256,320,384,448,512,576,640,704,768,832,896,960},{32,96,1..., dimensions={0}, use_global_device_ids=true | all-gather | bytes 557056 | tf_op jit(solution)/shard_map/all_gather | solution.py:156
  51.2 2.6 %collective-permute-start = (bf16[16,64,256]{2,1,0:T(8,128)(2,1)S(1)}, bf16[16,64,256]{2,1,0:T(8,128)(2,1)S(1)}, u32[]{:S(2)}, u32[]{:S(2)}) collective-permute-start(bf16[16,64,256]{2,1,0:T(8,128)(2,1)S(1)} %bitcast.10), channel_id=1, source_target_pairs={{0,32},{32,0},{64,96},{96,64},{128,160},{160,128},{192,224},{224,1... | collective-permute-start | bytes 1572872 | tf_op jit(solution)/shard_map/ppermute | solution.py:157
  53.8 0.0 copy-start.4
  54.5 0.0 copy-start.3
  54.5 0.0 copy-done.4
  54.5 0.7 copy-done.3
  55.1 0.0 copy-start
  55.1 1.1 copy-done
  56.3 0.1 shard_map.91
  56.3 0.0 copy-start.5
  56.3 0.0 copy-start.6
  56.4 0.6 copy-done.5
  57.0 0.0 copy-done.6
  57.0 0.1 concatenate.3.facts
  57.1 5.2 %collective-permute-done.other = bf16[16,64,256]{2,1,0:T(8,128)(2,1)S(1)} collective-permute-done((bf16[16,64,256]{2,1,0:T(8,128)(2,1)S(1)}, bf16[16,64,256]{2,1,0:T(8,128)(2,1)S(1)}, u32[]{:S(2)}, u32[]{:S(2)}) %collective-permute-start) | collective-permute-done | bytes 524320 | tf_op jit(solution)/shard_map/ppermute | solution.py:157
  62.2 1.1 shard_map.92
  63.3 17.8 %all_to_all.15.parts = bf16[16,128,256]{2,1,0:T(8,128)(2,1)S(1)} all-to-all(bf16[16,128,256]{2,1,0:T(8,128)(2,1)S(1)} %shard_map.92), channel_id=1, replica_groups={{0,2,4,6,8,10,12,14,16,18,20,22,24,26,28,30},{1,3,5,7,9,11,13,15,17,19,..., dimensions={0} | all-to-all | bytes 2097152 | tf_op jit(solution)/shard_map/all_to_all | solution.py:168
  81.1 0.0 copy-start.2
  81.1 0.7 shard_map.93
  81.9 1.9 %collective-permute-start.1 = (f32[64,256]{1,0:T(8,128)S(1)}, f32[64,256]{1,0:T(8,128)S(1)}, u32[]{:S(2)}, u32[]{:S(2)}) collective-permute-start(f32[64,256]{1,0:T(8,128)S(1)} %get-tuple-element.16), channel_id=1, source_target_pairs={{0,1},{1,0},{2,3},{3,2},{4,5},{5,4},{6,7},{7,6},{8,9},{9,8},{10,11... | collective-permute-start | bytes 196616 | tf_op jit(solution)/shard_map/ppermute | solution.py:173
  83.8 1.2 collective-permute-done.1.received
  85.0 0.0 copy-done.2
  85.0 0.2 shard_map.94
  85.2 14.8 %all_to_all.16.own = bf16[16,64,256]{2,1,0:T(8,128)(2,1)S(1)} all-to-all(bf16[16,64,256]{2,1,0:T(8,128)(2,1)S(1)} %shard_map.94), channel_id=1, replica_groups={{0,2,4,6,8,10,12,14,16,18,20,22,24,26,28,30},{1,3,5,7,9,11,13,15,17,19,..., dimensions={0} | all-to-all | bytes 1048576 | tf_op jit(solution)/shard_map/all_to_all | solution.py:176
  100.0 1.9 %collective-permute-start.2 = (bf16[16,64,256]{2,1,0:T(8,128)(2,1)S(1)}, bf16[16,64,256]{2,1,0:T(8,128)(2,1)S(1)}, u32[]{:S(2)}, u32[]{:S(2)}) collective-permute-start(bf16[16,64,256]{2,1,0:T(8,128)(2,1)S(1)} %all_to_all.16.own), channel_id=1, source_target_pairs={{0,1},{1,0},{2,3},{3,2},{4,5},{5,4},{6,7},{7,6},{8,9},{9,8},{10,11... | collective-permute-start | bytes 1572872 | tf_op jit(solution)/shard_map/ppermute | solution.py:177
  101.9 1.9 %collective-permute-done.2.other = bf16[16,64,256]{2,1,0:T(8,128)(2,1)S(1)} collective-permute-done((bf16[16,64,256]{2,1,0:T(8,128)(2,1)S(1)}, bf16[16,64,256]{2,1,0:T(8,128)(2,1)S(1)}, u32[]{:S(2)}, u32[]{:S(2)}) %collective-permute-start.2) | collective-permute-done | bytes 524320 | tf_op jit(solution)/shard_map/ppermute | solution.py:177
  103.8 1.1 shard_map.95
  105.0 2.2 %collective-permute-start.3 = (bf16[8,64,256]{2,1,0:T(8,128)(2,1)S(1)}, bf16[8,64,256]{2,1,0:T(8,128)(2,1)S(1)}, u32[]{:S(2)}, u32[]{:S(2)}) collective-permute-start(bf16[8,64,256]{2,1,0:T(8,128)(2,1)S(1)} %get-tuple-element.19), channel_id=1, source_target_pairs={{0,64},{32,992},{64,128},{96,32},{128,192},{160,96},{192,256},{224... | collective-permute-start | bytes 786440 | tf_op jit(solution)/shard_map/ppermute | solution.py:186
  107.1 4.9 %collective-permute-start.4 = (bf16[8,64,256]{2,1,0:T(8,128)(2,1)S(1)}, bf16[8,64,256]{2,1,0:T(8,128)(2,1)S(1)}, u32[]{:S(2)}, u32[]{:S(2)}) collective-permute-start(bf16[8,64,256]{2,1,0:T(8,128)(2,1)S(1)} %get-tuple-element.20), channel_id=1, source_target_pairs={{0,32},{32,64},{64,96},{96,128},{128,160},{160,192},{192,224},{224... | collective-permute-start | bytes 786440 | tf_op jit(solution)/shard_map/ppermute | solution.py:187
  112.0 3.1 %collective-permute-start.5 = (bf16[8,64,256]{2,1,0:T(8,128)(2,1)S(1)}, bf16[8,64,256]{2,1,0:T(8,128)(2,1)S(1)}, u32[]{:S(2)}, u32[]{:S(2)}) collective-permute-start(bf16[8,64,256]{2,1,0:T(8,128)(2,1)S(1)} %get-tuple-element.21), channel_id=1, source_target_pairs={{0,992},{32,0},{64,32},{96,64},{128,96},{160,128},{192,160},{224,1... | collective-permute-start | bytes 786440 | tf_op jit(solution)/shard_map/ppermute | solution.py:188
  115.1 3.1 %collective-permute-done.3 = bf16[8,64,256]{2,1,0:T(8,128)(2,1)S(1)} collective-permute-done((bf16[8,64,256]{2,1,0:T(8,128)(2,1)S(1)}, bf16[8,64,256]{2,1,0:T(8,128)(2,1)S(1)}, u32[]{:S(2)}, u32[]{:S(2)}) %collective-permute-start.3) | collective-permute-done | bytes 262176 | tf_op jit(solution)/shard_map/ppermute | solution.py:186
  118.2 4.8 %collective-permute-done.4 = bf16[8,64,256]{2,1,0:T(8,128)(2,1)S(1)} collective-permute-done((bf16[8,64,256]{2,1,0:T(8,128)(2,1)S(1)}, bf16[8,64,256]{2,1,0:T(8,128)(2,1)S(1)}, u32[]{:S(2)}, u32[]{:S(2)}) %collective-permute-start.4) | collective-permute-done | bytes 262176 | tf_op jit(solution)/shard_map/ppermute | solution.py:187
  122.9 0.0 collective-permute-done.5
  123.0 0.1 add_convert_fusion
  123.1 0.0 copy-start.1
  123.1 53.7 %all_to_all.17.parts = bf16[8,64,256]{2,1,0:T(8,128)(2,1)S(1)} all-to-all(bf16[8,64,256]{2,1,0:T(8,128)(2,1)S(1)} %add_convert_fusion), channel_id=1, replica_groups={{0,128,256,384,512,640,768,896},{32,160,288,416,544,672,800,928},{64,19..., dimensions={0} | all-to-all | bytes 524288 | tf_op jit(solution)/shard_map/all_to_all | solution.py:190
  176.8 0.0 copy-done.1
  176.8 0.8 shard_map.96
Async XLA Ops:
  51.2 11.1 %collective-permute-start = (bf16[16,64,256]{2,1,0:T(8,128)(2,1)S(1)}, bf16[16,64,256]{2,1,0:T(8,128)(2,1)S(1)}, u32[]{:S(2)}, u32[]{:S(2)}) collective-permute-start(bf16[16,64,256]{2,1,0:T(8,128)(2,1)S(1)} %bitcast.10), channel_id=1, source_target_pairs={{0,32},{32,0},{64,96},{96,64},{128,160},{160,128},{192,224},{224,1... | collective-permute-start | bytes 1572872 | tf_op jit(solution)/shard_map/ppermute | solution.py:157
  53.8 0.7 copy-start.4
  54.5 0.7 copy-start.3
  55.1 1.1 copy-start
  56.3 0.7 copy-start.5
  56.3 0.7 copy-start.6
  81.1 3.9 %copy-start.2 = (bf16[256,256]{1,0:T(8,128)(2,1)S(1)}, bf16[256,256]{1,0:T(8,128)(2,1)}, u32[]{:S(2)}) copy-start(bf16[256,256]{1,0:T(8,128)(2,1)} %weight.2) | copy-start | bytes 393220
  81.9 3.1 %collective-permute-start.1 = (f32[64,256]{1,0:T(8,128)S(1)}, f32[64,256]{1,0:T(8,128)S(1)}, u32[]{:S(2)}, u32[]{:S(2)}) collective-permute-start(f32[64,256]{1,0:T(8,128)S(1)} %get-tuple-element.16), channel_id=1, source_target_pairs={{0,1},{1,0},{2,3},{3,2},{4,5},{5,4},{6,7},{7,6},{8,9},{9,8},{10,11... | collective-permute-start | bytes 196616 | tf_op jit(solution)/shard_map/ppermute | solution.py:173
  100.0 3.8 %collective-permute-start.2 = (bf16[16,64,256]{2,1,0:T(8,128)(2,1)S(1)}, bf16[16,64,256]{2,1,0:T(8,128)(2,1)S(1)}, u32[]{:S(2)}, u32[]{:S(2)}) collective-permute-start(bf16[16,64,256]{2,1,0:T(8,128)(2,1)S(1)} %all_to_all.16.own), channel_id=1, source_target_pairs={{0,1},{1,0},{2,3},{3,2},{4,5},{5,4},{6,7},{7,6},{8,9},{9,8},{10,11... | collective-permute-start | bytes 1572872 | tf_op jit(solution)/shard_map/ppermute | solution.py:177
  105.0 13.2 %collective-permute-start.3 = (bf16[8,64,256]{2,1,0:T(8,128)(2,1)S(1)}, bf16[8,64,256]{2,1,0:T(8,128)(2,1)S(1)}, u32[]{:S(2)}, u32[]{:S(2)}) collective-permute-start(bf16[8,64,256]{2,1,0:T(8,128)(2,1)S(1)} %get-tuple-element.19), channel_id=1, source_target_pairs={{0,64},{32,992},{64,128},{96,32},{128,192},{160,96},{192,256},{224... | collective-permute-start | bytes 786440 | tf_op jit(solution)/shard_map/ppermute | solution.py:186
  107.1 15.8 %collective-permute-start.4 = (bf16[8,64,256]{2,1,0:T(8,128)(2,1)S(1)}, bf16[8,64,256]{2,1,0:T(8,128)(2,1)S(1)}, u32[]{:S(2)}, u32[]{:S(2)}) collective-permute-start(bf16[8,64,256]{2,1,0:T(8,128)(2,1)S(1)} %get-tuple-element.20), channel_id=1, source_target_pairs={{0,32},{32,64},{64,96},{96,128},{128,160},{160,192},{192,224},{224... | collective-permute-start | bytes 786440 | tf_op jit(solution)/shard_map/ppermute | solution.py:187
  112.0 11.0 %collective-permute-start.5 = (bf16[8,64,256]{2,1,0:T(8,128)(2,1)S(1)}, bf16[8,64,256]{2,1,0:T(8,128)(2,1)S(1)}, u32[]{:S(2)}, u32[]{:S(2)}) collective-permute-start(bf16[8,64,256]{2,1,0:T(8,128)(2,1)S(1)} %get-tuple-element.21), channel_id=1, source_target_pairs={{0,992},{32,0},{64,32},{96,64},{128,96},{160,128},{192,160},{224,1... | collective-permute-start | bytes 786440 | tf_op jit(solution)/shard_map/ppermute | solution.py:188
  123.1 53.7 %copy-start.1 = (bf16[256,256]{1,0:T(8,128)(2,1)S(1)}, bf16[256,256]{1,0:T(8,128)(2,1)}, u32[]{:S(2)}) copy-start(bf16[256,256]{1,0:T(8,128)(2,1)} %weight.3) | copy-start | bytes 393220

commit v6 on v4

--- a/solution.py
+++ b/solution.py
@@ -30,7 +30,9 @@
 
 def quartets(size):
     quads = size // 4
-    return [[4 * j + (g if j < quads // 2 else g ^ 1) for j in range(quads)] for g in range(4)]
+    return [
+        [4 * j + (g if j < quads // 2 else g ^ 1) for j in reversed(range(quads))] for g in range(4)
+    ]
 
 
 def swap(size):
@@ -98,7 +100,7 @@
         for j in range(quads):
             side = lax.rem(g + (0 if j < quads // 2 else 1), 2)
             offset = pl.multiple_of(side * half, half)
-            ref[j] = acc[2 * j + g // 2, pl.ds(offset, half), :].astype(ref.dtype)
+            ref[quads - 1 - j] = acc[2 * j + g // 2, pl.ds(offset, half), :].astype(ref.dtype)
 
 
 def dense_kernel(layer, parts, weight, bias, out):

time: 178 us -> 176 us (0.989)
  the two profiles are of different devices: /device:TPU:6 before, /device:TPU:32 now
where the time goes in v6:
time: 176 us
  blocking collectives  135 us (77%)
  waiting for transfers between devices  17.4 us (10%)
  starting transfers between devices  15.1 us (9%)
  Pallas kernels  4.81 us (3%)
  local copies, waits for them, and re-layouts  2.55 us (1%)
    all_to_all x1, blocking collectives, per_device(): terms = lax.all_to_all(summed, ROW, 0, 0, axis_index_groups=quartets(rows))  52.4 us
    all_gather x1, blocking collectives, per_device(): same = lax.all_gather(features, ROW, axis_index_groups=strided(rows, 2))  50 us
    all_to_all x1, blocking collectives, per_device(): lax.all_to_all(summed, COL, 0, 0, axis_index_groups=strided(cols, 2))  18.9 us
    all_to_all x1, blocking collectives, per_device(): mine = lax.all_to_all(copies, COL, 0, 0, axis_index_groups=strided(cols, 2))  14 us
    ppermute x1, waiting for transfers between devices, per_device(): two = lax.ppermute(two, ROW, hop_two(rows))  5.21 us
    ppermute x1, waiting for transfers between devices, per_device(): other = lax.ppermute(same, ROW, swap(rows))  4.54 us
    ppermute x1, waiting for transfers between devices, per_device(): up = lax.ppermute(up, ROW, shift(rows, 1))  3.88 us
  transfers between devices with their start and end apart: 6, of which 5 were waited for; matrix products, arithmetic and copies ran while one was open for 0% of the time, Pallas kernels for 0%

profile of v6, /device:TPU:32, one launch (start us, length us, event | category | flops | bytes accessed | tf_op | source)
XLA Modules:
  0.0 176.2 jit_solution(13626208831638851635)
XLA Ops:
  0.0 50.0 %all-gather = bf16[1024,256]{1,0:T(8,128)(2,1)S(1)} all-gather(bf16[64,256]{1,0:T(8,128)(2,1)} %param.9), channel_id=2, replica_groups={{0,64,128,192,256,320,384,448,512,576,640,704,768,832,896,960},{32,96,1..., dimensions={0}, use_global_device_ids=true | all-gather | bytes 557056 | tf_op jit(solution)/shard_map/all_gather | solution.py:163
  50.0 3.2 %collective-permute-start = (bf16[16,64,256]{2,1,0:T(8,128)(2,1)S(1)}, bf16[16,64,256]{2,1,0:T(8,128)(2,1)S(1)}, u32[]{:S(2)}, u32[]{:S(2)}) collective-permute-start(bf16[16,64,256]{2,1,0:T(8,128)(2,1)S(1)} %bitcast.10), channel_id=1, source_target_pairs={{0,32},{32,0},{64,96},{96,64},{128,160},{160,128},{192,224},{224,1... | collective-permute-start | bytes 1572872 | tf_op jit(solution)/shard_map/ppermute | solution.py:164
  53.2 0.0 copy-start.4
  53.9 0.0 copy-start.3
  53.9 0.0 copy-done.4
  53.9 0.7 copy-done.3
  54.5 0.0 copy-start
  54.5 1.1 copy-done
  55.7 0.1 shard_map.91
  55.7 0.0 copy-start.5
  55.7 0.0 copy-start.6
  55.8 0.6 copy-done.5
  56.4 0.0 copy-done.6
  56.4 0.1 concatenate.3.facts
  56.5 4.5 %collective-permute-done.other = bf16[16,64,256]{2,1,0:T(8,128)(2,1)S(1)} collective-permute-done((bf16[16,64,256]{2,1,0:T(8,128)(2,1)S(1)}, bf16[16,64,256]{2,1,0:T(8,128)(2,1)S(1)}, u32[]{:S(2)}, u32[]{:S(2)}) %collective-permute-start) | collective-permute-done | bytes 524320 | tf_op jit(solution)/shard_map/ppermute | solution.py:164
  61.0 1.8 %shard_map.92 = (f32[16,64,256]{2,1,0:T(8,128)S(1)}, bf16[16,64,256]{2,1,0:T(8,128)(2,1)S(1)}) custom-call(s32[51]{0:T(128)S(1)} %concatenate.3.facts, bf16[24,128,128]{2,1,0:T(8,128)(2,1)S(1)} %get-tuple-element.14.values, bf16[16,64,256]{2,1,0:T(8,128)(2,1)S(1)} %bitcast.12, bf16[16,64,256]{2,1,0:T(8,128)(2,1)S(1)} %collective-permute-done.other), custom_call_target="tpu_custom_call" | custom-call | tf_op jit(solution)/shard_map/pallas_call | solution.py:171
  62.8 1.9 %collective-permute-start.1 = (bf16[16,64,256]{2,1,0:T(8,128)(2,1)S(1)}, bf16[16,64,256]{2,1,0:T(8,128)(2,1)S(1)}, u32[]{:S(2)}, u32[]{:S(2)}) collective-permute-start(bf16[16,64,256]{2,1,0:T(8,128)(2,1)S(1)} %get-tuple-element.16), channel_id=1, source_target_pairs={{0,1},{1,0},{2,3},{3,2},{4,5},{5,4},{6,7},{7,6},{8,9},{9,8},{10,11... | collective-permute-start | bytes 1572872 | tf_op jit(solution)/shard_map/ppermute | solution.py:175
  64.8 1.9 %collective-permute-done.1 = bf16[16,64,256]{2,1,0:T(8,128)(2,1)S(1)} collective-permute-done((bf16[16,64,256]{2,1,0:T(8,128)(2,1)S(1)}, bf16[16,64,256]{2,1,0:T(8,128)(2,1)S(1)}, u32[]{:S(2)}, u32[]{:S(2)}) %collective-permute-start.1) | collective-permute-done | bytes 524320 | tf_op jit(solution)/shard_map/ppermute | solution.py:175
  66.6 0.1 add_convert_fusion
  66.8 0.0 copy-start.2
  66.8 18.9 %all_to_all.15.parts = bf16[16,64,256]{2,1,0:T(8,128)(2,1)S(1)} all-to-all(bf16[16,64,256]{2,1,0:T(8,128)(2,1)S(1)} %add_convert_fusion), channel_id=1, replica_groups={{0,2,4,6,8,10,12,14,16,18,20,22,24,26,28,30},{1,3,5,7,9,11,13,15,17,19,..., dimensions={0} | all-to-all | bytes 1048576 | tf_op jit(solution)/shard_map/all_to_all | solution.py:176
  85.7 0.0 copy-done.2
  85.7 0.2 shard_map.93
  85.9 14.0 %all_to_all.16.own = bf16[16,64,256]{2,1,0:T(8,128)(2,1)S(1)} all-to-all(bf16[16,64,256]{2,1,0:T(8,128)(2,1)S(1)} %shard_map.93), channel_id=1, replica_groups={{0,2,4,6,8,10,12,14,16,18,20,22,24,26,28,30},{1,3,5,7,9,11,13,15,17,19,..., dimensions={0} | all-to-all | bytes 1048576 | tf_op jit(solution)/shard_map/all_to_all | solution.py:181
  99.9 1.9 %collective-permute-start.2 = (bf16[16,64,256]{2,1,0:T(8,128)(2,1)S(1)}, bf16[16,64,256]{2,1,0:T(8,128)(2,1)S(1)}, u32[]{:S(2)}, u32[]{:S(2)}) collective-permute-start(bf16[16,64,256]{2,1,0:T(8,128)(2,1)S(1)} %all_to_all.16.own), channel_id=1, source_target_pairs={{0,1},{1,0},{2,3},{3,2},{4,5},{5,4},{6,7},{7,6},{8,9},{9,8},{10,11... | collective-permute-start | bytes 1572872 | tf_op jit(solution)/shard_map/ppermute | solution.py:182
  101.8 1.9 %collective-permute-done.2.other = bf16[16,64,256]{2,1,0:T(8,128)(2,1)S(1)} collective-permute-done((bf16[16,64,256]{2,1,0:T(8,128)(2,1)S(1)}, bf16[16,64,256]{2,1,0:T(8,128)(2,1)S(1)}, u32[]{:S(2)}, u32[]{:S(2)}) %collective-permute-start.2) | collective-permute-done | bytes 524320 | tf_op jit(solution)/shard_map/ppermute | solution.py:182
  103.7 1.9 %shard_map.94 = (f32[8,64,256]{2,1,0:T(8,128)S(1)}, bf16[8,64,256]{2,1,0:T(8,128)(2,1)S(1)}, bf16[8,64,256]{2,1,0:T(8,128)(2,1)S(1)}, bf16[8,64,256]{2,1,0:T(8,128)(2,1)S(1)}) custom-call(s32[51]{0:T(128)S(1)} %concatenate.3.facts, bf16[24,128,128]{2,1,0:T(8,128)(2,1)S(1)} %get-tuple-element.14.values, bf16[16,64,256]{2,1,0:T(8,128)(2,1)S(1)} %all_to_all.16.own, ...), custom_call_target="tpu_custom_call" | custom-call | tf_op jit(solution)/shard_map/pallas_call | solution.py:184
  105.6 2.2 %collective-permute-start.3 = (bf16[8,64,256]{2,1,0:T(8,128)(2,1)S(1)}, bf16[8,64,256]{2,1,0:T(8,128)(2,1)S(1)}, u32[]{:S(2)}, u32[]{:S(2)}) collective-permute-start(bf16[8,64,256]{2,1,0:T(8,128)(2,1)S(1)} %get-tuple-element.19), channel_id=1, source_target_pairs={{0,960},{32,96},{64,0},{96,160},{128,64},{160,224},{192,128},{224,... | collective-permute-start | bytes 786440 | tf_op jit(solution)/shard_map/ppermute | solution.py:191
  107.8 3.4 %collective-permute-start.4 = (bf16[8,64,256]{2,1,0:T(8,128)(2,1)S(1)}, bf16[8,64,256]{2,1,0:T(8,128)(2,1)S(1)}, u32[]{:S(2)}, u32[]{:S(2)}) collective-permute-start(bf16[8,64,256]{2,1,0:T(8,128)(2,1)S(1)} %get-tuple-element.20), channel_id=1, source_target_pairs={{0,32},{32,64},{64,96},{96,128},{128,160},{160,192},{192,224},{224... | collective-permute-start | bytes 786440 | tf_op jit(solution)/shard_map/ppermute | solution.py:192
  111.2 2.5 %collective-permute-start.5 = (bf16[8,64,256]{2,1,0:T(8,128)(2,1)S(1)}, bf16[8,64,256]{2,1,0:T(8,128)(2,1)S(1)}, u32[]{:S(2)}, u32[]{:S(2)}) collective-permute-start(bf16[8,64,256]{2,1,0:T(8,128)(2,1)S(1)} %get-tuple-element.21), channel_id=1, source_target_pairs={{0,992},{32,0},{64,32},{96,64},{128,96},{160,128},{192,160},{224,1... | collective-permute-start | bytes 786440 | tf_op jit(solution)/shard_map/ppermute | solution.py:193
  113.7 5.2 %collective-permute-done.3 = bf16[8,64,256]{2,1,0:T(8,128)(2,1)S(1)} collective-permute-done((bf16[8,64,256]{2,1,0:T(8,128)(2,1)S(1)}, bf16[8,64,256]{2,1,0:T(8,128)(2,1)S(1)}, u32[]{:S(2)}, u32[]{:S(2)}) %collective-permute-start.3) | collective-permute-done | bytes 262176 | tf_op jit(solution)/shard_map/ppermute | solution.py:191
  118.9 3.9 %collective-permute-done.4 = bf16[8,64,256]{2,1,0:T(8,128)(2,1)S(1)} collective-permute-done((bf16[8,64,256]{2,1,0:T(8,128)(2,1)S(1)}, bf16[8,64,256]{2,1,0:T(8,128)(2,1)S(1)}, u32[]{:S(2)}, u32[]{:S(2)}) %collective-permute-start.4) | collective-permute-done | bytes 262176 | tf_op jit(solution)/shard_map/ppermute | solution.py:192
  122.8 0.0 collective-permute-done.5
  122.8 0.1 add_convert_fusion.1
  122.9 0.0 copy-start.1
  122.9 52.4 %all_to_all.17.parts = bf16[8,64,256]{2,1,0:T(8,128)(2,1)S(1)} all-to-all(bf16[8,64,256]{2,1,0:T(8,128)(2,1)S(1)} %add_convert_fusion.1), channel_id=1, replica_groups={{928,800,672,544,384,256,128,0},{896,768,640,512,416,288,160,32},{992,8..., dimensions={0} | all-to-all | bytes 524288 | tf_op jit(solution)/shard_map/all_to_all | solution.py:195
  175.3 0.0 copy-done.1
  175.3 0.8 shard_map.95
Async XLA Ops:
  50.0 11.1 %collective-permute-start = (bf16[16,64,256]{2,1,0:T(8,128)(2,1)S(1)}, bf16[16,64,256]{2,1,0:T(8,128)(2,1)S(1)}, u32[]{:S(2)}, u32[]{:S(2)}) collective-permute-start(bf16[16,64,256]{2,1,0:T(8,128)(2,1)S(1)} %bitcast.10), channel_id=1, source_target_pairs={{0,32},{32,0},{64,96},{96,64},{128,160},{160,128},{192,224},{224,1... | collective-permute-start | bytes 1572872 | tf_op jit(solution)/shard_map/ppermute | solution.py:164
  53.2 0.7 copy-start.4
  53.9 0.7 copy-start.3
  54.5 1.1 copy-start
  55.7 0.7 copy-start.5
  55.7 0.7 copy-start.6
  62.8 3.8 %collective-permute-start.1 = (bf16[16,64,256]{2,1,0:T(8,128)(2,1)S(1)}, bf16[16,64,256]{2,1,0:T(8,128)(2,1)S(1)}, u32[]{:S(2)}, u32[]{:S(2)}) collective-permute-start(bf16[16,64,256]{2,1,0:T(8,128)(2,1)S(1)} %get-tuple-element.16), channel_id=1, source_target_pairs={{0,1},{1,0},{2,3},{3,2},{4,5},{5,4},{6,7},{7,6},{8,9},{9,8},{10,11... | collective-permute-start | bytes 1572872 | tf_op jit(solution)/shard_map/ppermute | solution.py:175
  66.8 18.9 %copy-start.2 = (bf16[256,256]{1,0:T(8,128)(2,1)S(1)}, bf16[256,256]{1,0:T(8,128)(2,1)}, u32[]{:S(2)}) copy-start(bf16[256,256]{1,0:T(8,128)(2,1)} %weight.2) | copy-start | bytes 393220
  99.9 3.8 %collective-permute-start.2 = (bf16[16,64,256]{2,1,0:T(8,128)(2,1)S(1)}, bf16[16,64,256]{2,1,0:T(8,128)(2,1)S(1)}, u32[]{:S(2)}, u32[]{:S(2)}) collective-permute-start(bf16[16,64,256]{2,1,0:T(8,128)(2,1)S(1)} %all_to_all.16.own), channel_id=1, source_target_pairs={{0,1},{1,0},{2,3},{3,2},{4,5},{5,4},{6,7},{7,6},{8,9},{9,8},{10,11... | collective-permute-start | bytes 1572872 | tf_op jit(solution)/shard_map/ppermute | solution.py:182
  105.6 13.3 %collective-permute-start.3 = (bf16[8,64,256]{2,1,0:T(8,128)(2,1)S(1)}, bf16[8,64,256]{2,1,0:T(8,128)(2,1)S(1)}, u32[]{:S(2)}, u32[]{:S(2)}) collective-permute-start(bf16[8,64,256]{2,1,0:T(8,128)(2,1)S(1)} %get-tuple-element.19), channel_id=1, source_target_pairs={{0,960},{32,96},{64,0},{96,160},{128,64},{160,224},{192,128},{224,... | collective-permute-start | bytes 786440 | tf_op jit(solution)/shard_map/ppermute | solution.py:191
  107.8 14.9 %collective-permute-start.4 = (bf16[8,64,256]{2,1,0:T(8,128)(2,1)S(1)}, bf16[8,64,256]{2,1,0:T(8,128)(2,1)S(1)}, u32[]{:S(2)}, u32[]{:S(2)}) collective-permute-start(bf16[8,64,256]{2,1,0:T(8,128)(2,1)S(1)} %get-tuple-element.20), channel_id=1, source_target_pairs={{0,32},{32,64},{64,96},{96,128},{128,160},{160,192},{192,224},{224... | collective-permute-start | bytes 786440 | tf_op jit(solution)/shard_map/ppermute | solution.py:192
  111.2 11.6 %collective-permute-start.5 = (bf16[8,64,256]{2,1,0:T(8,128)(2,1)S(1)}, bf16[8,64,256]{2,1,0:T(8,128)(2,1)S(1)}, u32[]{:S(2)}, u32[]{:S(2)}) collective-permute-start(bf16[8,64,256]{2,1,0:T(8,128)(2,1)S(1)} %get-tuple-element.21), channel_id=1, source_target_pairs={{0,992},{32,0},{64,32},{96,64},{128,96},{160,128},{192,160},{224,1... | collective-permute-start | bytes 786440 | tf_op jit(solution)/shard_map/ppermute | solution.py:193
  122.9 52.4 %copy-start.1 = (bf16[256,256]{1,0:T(8,128)(2,1)S(1)}, bf16[256,256]{1,0:T(8,128)(2,1)}, u32[]{:S(2)}) copy-start(bf16[256,256]{1,0:T(8,128)(2,1)} %weight.3) | copy-start | bytes 393220

commit v7 on v6

--- a/solution.py
+++ b/solution.py
@@ -31,7 +31,8 @@
 def quartets(size):
     quads = size // 4
     return [
-        [4 * j + (g if j < quads // 2 else g ^ 1) for j in reversed(range(quads))] for g in range(4)
+        [4 * j + (g if j < quads // 2 else g ^ 1) for j in range(quads)][:: 1 if g % 2 else -1]
+        for g in range(4)
     ]
 
 
@@ -100,7 +101,8 @@
         for j in range(quads):
             side = lax.rem(g + (0 if j < quads // 2 else 1), 2)
             offset = pl.multiple_of(side * half, half)
-            ref[quads - 1 - j] = acc[2 * j + g // 2, pl.ds(offset, half), :].astype(ref.dtype)
+            slot = jnp.where(lax.rem(g, 2) == 0, quads - 1 - j, j)
+            ref[slot] = acc[2 * j + g // 2, pl.ds(offset, half), :].astype(ref.dtype)
 
 
 def dense_kernel(layer, parts, weight, bias, out):

time: 176 us -> 177 us (level)
  no operation moved by 1% of the time
where the time goes in v7:
time: 177 us; the launch traced here: 176 us
  blocking collectives  134 us (76%)
  waiting for transfers between devices  18.1 us (10%)
  starting transfers between devices  14.8 us (8%)
  Pallas kernels  5.33 us (3%)
  local copies, waits for them, and re-layouts  2.55 us (1%)
    all_to_all x1, blocking collectives, per_device(): terms = lax.all_to_all(summed, ROW, 0, 0, axis_index_groups=quartets(rows))  51.3 us
    all_gather x1, blocking collectives, per_device(): same = lax.all_gather(features, ROW, axis_index_groups=strided(rows, 2))  50 us
    all_to_all x1, blocking collectives, per_device(): lax.all_to_all(summed, COL, 0, 0, axis_index_groups=strided(cols, 2))  18.8 us
    all_to_all x1, blocking collectives, per_device(): mine = lax.all_to_all(copies, COL, 0, 0, axis_index_groups=strided(cols, 2))  14 us
    ppermute x1, waiting for transfers between devices, per_device(): two = lax.ppermute(two, ROW, hop_two(rows))  5.45 us
    ppermute x1, waiting for transfers between devices, per_device(): other = lax.ppermute(same, ROW, swap(rows))  4.54 us
    ppermute x1, waiting for transfers between devices, per_device(): up = lax.ppermute(up, ROW, shift(rows, 1))  4.35 us
  transfers between devices with their start and end apart: 6, of which 5 were waited for; matrix products, arithmetic and copies ran while one was open for 0% of the time, Pallas kernels for 0%

profile of v7, /device:TPU:32, one launch (start us, length us, event | category | flops | bytes accessed | tf_op | source)
XLA Modules:
  0.0 176.0 jit_solution(7632682006141595382)
XLA Ops:
  0.0 50.0 %all-gather = bf16[1024,256]{1,0:T(8,128)(2,1)S(1)} all-gather(bf16[64,256]{1,0:T(8,128)(2,1)} %param.9), channel_id=2, replica_groups={{0,64,128,192,256,320,384,448,512,576,640,704,768,832,896,960},{32,96,1..., dimensions={0}, use_global_device_ids=true | all-gather | bytes 557056 | tf_op jit(solution)/shard_map/all_gather | solution.py:165
  50.0 3.2 %collective-permute-start = (bf16[16,64,256]{2,1,0:T(8,128)(2,1)S(1)}, bf16[16,64,256]{2,1,0:T(8,128)(2,1)S(1)}, u32[]{:S(2)}, u32[]{:S(2)}) collective-permute-start(bf16[16,64,256]{2,1,0:T(8,128)(2,1)S(1)} %bitcast.10), channel_id=1, source_target_pairs={{0,32},{32,0},{64,96},{96,64},{128,160},{160,128},{192,224},{224,1... | collective-permute-start | bytes 1572872 | tf_op jit(solution)/shard_map/ppermute | solution.py:166
  53.2 0.0 copy-start.4
  53.9 0.0 copy-start.3
  53.9 0.0 copy-done.4
  53.9 0.7 copy-done.3
  54.5 0.0 copy-start
  54.5 1.1 copy-done
  55.7 0.1 shard_map.91
  55.7 0.0 copy-start.5
  55.7 0.0 copy-start.6
  55.8 0.6 copy-done.5
  56.4 0.0 copy-done.6
  56.4 0.1 concatenate.3.facts
  56.5 4.5 %collective-permute-done.other = bf16[16,64,256]{2,1,0:T(8,128)(2,1)S(1)} collective-permute-done((bf16[16,64,256]{2,1,0:T(8,128)(2,1)S(1)}, bf16[16,64,256]{2,1,0:T(8,128)(2,1)S(1)}, u32[]{:S(2)}, u32[]{:S(2)}) %collective-permute-start) | collective-permute-done | bytes 524320 | tf_op jit(solution)/shard_map/ppermute | solution.py:166
  61.0 2.0 %shard_map.92 = (f32[16,64,256]{2,1,0:T(8,128)S(1)}, bf16[16,64,256]{2,1,0:T(8,128)(2,1)S(1)}) custom-call(s32[51]{0:T(128)S(1)} %concatenate.3.facts, bf16[24,128,128]{2,1,0:T(8,128)(2,1)S(1)} %get-tuple-element.14.values, bf16[16,64,256]{2,1,0:T(8,128)(2,1)S(1)} %bitcast.12, bf16[16,64,256]{2,1,0:T(8,128)(2,1)S(1)} %collective-permute-done.other), custom_call_target="tpu_custom_call" | custom-call | tf_op jit(solution)/shard_map/pallas_call | solution.py:173
  63.1 1.9 %collective-permute-start.1 = (bf16[16,64,256]{2,1,0:T(8,128)(2,1)S(1)}, bf16[16,64,256]{2,1,0:T(8,128)(2,1)S(1)}, u32[]{:S(2)}, u32[]{:S(2)}) collective-permute-start(bf16[16,64,256]{2,1,0:T(8,128)(2,1)S(1)} %get-tuple-element.16), channel_id=1, source_target_pairs={{0,1},{1,0},{2,3},{3,2},{4,5},{5,4},{6,7},{7,6},{8,9},{9,8},{10,11... | collective-permute-start | bytes 1572872 | tf_op jit(solution)/shard_map/ppermute | solution.py:177
  65.0 1.9 %collective-permute-done.1 = bf16[16,64,256]{2,1,0:T(8,128)(2,1)S(1)} collective-permute-done((bf16[16,64,256]{2,1,0:T(8,128)(2,1)S(1)}, bf16[16,64,256]{2,1,0:T(8,128)(2,1)S(1)}, u32[]{:S(2)}, u32[]{:S(2)}) %collective-permute-start.1) | collective-permute-done | bytes 524320 | tf_op jit(solution)/shard_map/ppermute | solution.py:177
  66.9 0.1 add_convert_fusion
  67.0 0.0 copy-start.2
  67.0 18.8 %all_to_all.15.parts = bf16[16,64,256]{2,1,0:T(8,128)(2,1)S(1)} all-to-all(bf16[16,64,256]{2,1,0:T(8,128)(2,1)S(1)} %add_convert_fusion), channel_id=1, replica_groups={{0,2,4,6,8,10,12,14,16,18,20,22,24,26,28,30},{1,3,5,7,9,11,13,15,17,19,..., dimensions={0} | all-to-all | bytes 1048576 | tf_op jit(solution)/shard_map/all_to_all | solution.py:178
  85.8 0.0 copy-done.2
  85.8 0.2 shard_map.93
  86.1 14.0 %all_to_all.16.own = bf16[16,64,256]{2,1,0:T(8,128)(2,1)S(1)} all-to-all(bf16[16,64,256]{2,1,0:T(8,128)(2,1)S(1)} %shard_map.93), channel_id=1, replica_groups={{0,2,4,6,8,10,12,14,16,18,20,22,24,26,28,30},{1,3,5,7,9,11,13,15,17,19,..., dimensions={0} | all-to-all | bytes 1048576 | tf_op jit(solution)/shard_map/all_to_all | solution.py:183
  100.1 1.9 %collective-permute-start.2 = (bf16[16,64,256]{2,1,0:T(8,128)(2,1)S(1)}, bf16[16,64,256]{2,1,0:T(8,128)(2,1)S(1)}, u32[]{:S(2)}, u32[]{:S(2)}) collective-permute-start(bf16[16,64,256]{2,1,0:T(8,128)(2,1)S(1)} %all_to_all.16.own), channel_id=1, source_target_pairs={{0,1},{1,0},{2,3},{3,2},{4,5},{5,4},{6,7},{7,6},{8,9},{9,8},{10,11... | collective-permute-start | bytes 1572872 | tf_op jit(solution)/shard_map/ppermute | solution.py:184
  102.0 1.9 %collective-permute-done.2.other = bf16[16,64,256]{2,1,0:T(8,128)(2,1)S(1)} collective-permute-done((bf16[16,64,256]{2,1,0:T(8,128)(2,1)S(1)}, bf16[16,64,256]{2,1,0:T(8,128)(2,1)S(1)}, u32[]{:S(2)}, u32[]{:S(2)}) %collective-permute-start.2) | collective-permute-done | bytes 524320 | tf_op jit(solution)/shard_map/ppermute | solution.py:184
  103.8 2.2 %shard_map.94 = (f32[8,64,256]{2,1,0:T(8,128)S(1)}, bf16[8,64,256]{2,1,0:T(8,128)(2,1)S(1)}, bf16[8,64,256]{2,1,0:T(8,128)(2,1)S(1)}, bf16[8,64,256]{2,1,0:T(8,128)(2,1)S(1)}) custom-call(s32[51]{0:T(128)S(1)} %concatenate.3.facts, bf16[24,128,128]{2,1,0:T(8,128)(2,1)S(1)} %get-tuple-element.14.values, bf16[16,64,256]{2,1,0:T(8,128)(2,1)S(1)} %all_to_all.16.own, ...), custom_call_target="tpu_custom_call" | custom-call | tf_op jit(solution)/shard_map/pallas_call | solution.py:186
  106.1 1.9 %collective-permute-start.3 = (bf16[8,64,256]{2,1,0:T(8,128)(2,1)S(1)}, bf16[8,64,256]{2,1,0:T(8,128)(2,1)S(1)}, u32[]{:S(2)}, u32[]{:S(2)}) collective-permute-start(bf16[8,64,256]{2,1,0:T(8,128)(2,1)S(1)} %get-tuple-element.19), channel_id=1, source_target_pairs={{0,960},{32,96},{64,0},{96,160},{128,64},{160,224},{192,128},{224,... | collective-permute-start | bytes 786440 | tf_op jit(solution)/shard_map/ppermute | solution.py:193
  108.0 3.0 %collective-permute-start.4 = (bf16[8,64,256]{2,1,0:T(8,128)(2,1)S(1)}, bf16[8,64,256]{2,1,0:T(8,128)(2,1)S(1)}, u32[]{:S(2)}, u32[]{:S(2)}) collective-permute-start(bf16[8,64,256]{2,1,0:T(8,128)(2,1)S(1)} %get-tuple-element.20), channel_id=1, source_target_pairs={{0,32},{32,64},{64,96},{96,128},{128,160},{160,192},{192,224},{224... | collective-permute-start | bytes 786440 | tf_op jit(solution)/shard_map/ppermute | solution.py:194
  111.0 2.9 %collective-permute-start.5 = (bf16[8,64,256]{2,1,0:T(8,128)(2,1)S(1)}, bf16[8,64,256]{2,1,0:T(8,128)(2,1)S(1)}, u32[]{:S(2)}, u32[]{:S(2)}) collective-permute-start(bf16[8,64,256]{2,1,0:T(8,128)(2,1)S(1)} %get-tuple-element.21), channel_id=1, source_target_pairs={{0,992},{32,0},{64,32},{96,64},{128,96},{160,128},{192,160},{224,1... | collective-permute-start | bytes 786440 | tf_op jit(solution)/shard_map/ppermute | solution.py:195
  113.9 5.5 %collective-permute-done.3 = bf16[8,64,256]{2,1,0:T(8,128)(2,1)S(1)} collective-permute-done((bf16[8,64,256]{2,1,0:T(8,128)(2,1)S(1)}, bf16[8,64,256]{2,1,0:T(8,128)(2,1)S(1)}, u32[]{:S(2)}, u32[]{:S(2)}) %collective-permute-start.3) | collective-permute-done | bytes 262176 | tf_op jit(solution)/shard_map/ppermute | solution.py:193
  119.3 4.4 %collective-permute-done.4 = bf16[8,64,256]{2,1,0:T(8,128)(2,1)S(1)} collective-permute-done((bf16[8,64,256]{2,1,0:T(8,128)(2,1)S(1)}, bf16[8,64,256]{2,1,0:T(8,128)(2,1)S(1)}, u32[]{:S(2)}, u32[]{:S(2)}) %collective-permute-start.4) | collective-permute-done | bytes 262176 | tf_op jit(solution)/shard_map/ppermute | solution.py:194
  123.7 0.0 collective-permute-done.5
  123.7 0.1 add_convert_fusion.1
  123.8 0.0 copy-start.1
  123.8 51.3 %all_to_all.17.parts = bf16[8,64,256]{2,1,0:T(8,128)(2,1)S(1)} all-to-all(bf16[8,64,256]{2,1,0:T(8,128)(2,1)S(1)} %add_convert_fusion.1), channel_id=1, replica_groups={{928,800,672,544,384,256,128,0},{32,160,288,416,512,640,768,896},{992,8..., dimensions={0} | all-to-all | bytes 524288 | tf_op jit(solution)/shard_map/all_to_all | solution.py:197
  175.2 0.0 copy-done.1
  175.2 0.8 shard_map.95
Async XLA Ops:
  50.0 11.1 %collective-permute-start = (bf16[16,64,256]{2,1,0:T(8,128)(2,1)S(1)}, bf16[16,64,256]{2,1,0:T(8,128)(2,1)S(1)}, u32[]{:S(2)}, u32[]{:S(2)}) collective-permute-start(bf16[16,64,256]{2,1,0:T(8,128)(2,1)S(1)} %bitcast.10), channel_id=1, source_target_pairs={{0,32},{32,0},{64,96},{96,64},{128,160},{160,128},{192,224},{224,1... | collective-permute-start | bytes 1572872 | tf_op jit(solution)/shard_map/ppermute | solution.py:166
  53.2 0.7 copy-start.4
  53.9 0.7 copy-start.3
  54.5 1.1 copy-start
  55.7 0.7 copy-start.5
  55.7 0.7 copy-start.6
  63.1 3.8 %collective-permute-start.1 = (bf16[16,64,256]{2,1,0:T(8,128)(2,1)S(1)}, bf16[16,64,256]{2,1,0:T(8,128)(2,1)S(1)}, u32[]{:S(2)}, u32[]{:S(2)}) collective-permute-start(bf16[16,64,256]{2,1,0:T(8,128)(2,1)S(1)} %get-tuple-element.16), channel_id=1, source_target_pairs={{0,1},{1,0},{2,3},{3,2},{4,5},{5,4},{6,7},{7,6},{8,9},{9,8},{10,11... | collective-permute-start | bytes 1572872 | tf_op jit(solution)/shard_map/ppermute | solution.py:177
  67.0 18.8 %copy-start.2 = (bf16[256,256]{1,0:T(8,128)(2,1)S(1)}, bf16[256,256]{1,0:T(8,128)(2,1)}, u32[]{:S(2)}) copy-start(bf16[256,256]{1,0:T(8,128)(2,1)} %weight.2) | copy-start | bytes 393220
  100.1 3.8 %collective-permute-start.2 = (bf16[16,64,256]{2,1,0:T(8,128)(2,1)S(1)}, bf16[16,64,256]{2,1,0:T(8,128)(2,1)S(1)}, u32[]{:S(2)}, u32[]{:S(2)}) collective-permute-start(bf16[16,64,256]{2,1,0:T(8,128)(2,1)S(1)} %all_to_all.16.own), channel_id=1, source_target_pairs={{0,1},{1,0},{2,3},{3,2},{4,5},{5,4},{6,7},{7,6},{8,9},{9,8},{10,11... | collective-permute-start | bytes 1572872 | tf_op jit(solution)/shard_map/ppermute | solution.py:184
  106.1 13.2 %collective-permute-start.3 = (bf16[8,64,256]{2,1,0:T(8,128)(2,1)S(1)}, bf16[8,64,256]{2,1,0:T(8,128)(2,1)S(1)}, u32[]{:S(2)}, u32[]{:S(2)}) collective-permute-start(bf16[8,64,256]{2,1,0:T(8,128)(2,1)S(1)} %get-tuple-element.19), channel_id=1, source_target_pairs={{0,960},{32,96},{64,0},{96,160},{128,64},{160,224},{192,128},{224,... | collective-permute-start | bytes 786440 | tf_op jit(solution)/shard_map/ppermute | solution.py:193
  108.0 15.7 %collective-permute-start.4 = (bf16[8,64,256]{2,1,0:T(8,128)(2,1)S(1)}, bf16[8,64,256]{2,1,0:T(8,128)(2,1)S(1)}, u32[]{:S(2)}, u32[]{:S(2)}) collective-permute-start(bf16[8,64,256]{2,1,0:T(8,128)(2,1)S(1)} %get-tuple-element.20), channel_id=1, source_target_pairs={{0,32},{32,64},{64,96},{96,128},{128,160},{160,192},{192,224},{224... | collective-permute-start | bytes 786440 | tf_op jit(solution)/shard_map/ppermute | solution.py:194
  111.0 12.7 %collective-permute-start.5 = (bf16[8,64,256]{2,1,0:T(8,128)(2,1)S(1)}, bf16[8,64,256]{2,1,0:T(8,128)(2,1)S(1)}, u32[]{:S(2)}, u32[]{:S(2)}) collective-permute-start(bf16[8,64,256]{2,1,0:T(8,128)(2,1)S(1)} %get-tuple-element.21), channel_id=1, source_target_pairs={{0,992},{32,0},{64,32},{96,64},{128,96},{160,128},{192,160},{224,1... | collective-permute-start | bytes 786440 | tf_op jit(solution)/shard_map/ppermute | solution.py:195
  123.8 51.3 %copy-start.1 = (bf16[256,256]{1,0:T(8,128)(2,1)S(1)}, bf16[256,256]{1,0:T(8,128)(2,1)}, u32[]{:S(2)}) copy-start(bf16[256,256]{1,0:T(8,128)(2,1)} %weight.3) | copy-start | bytes 393220
